TPU v7x, 128 devices: a whole 4x4x4 slice. The times are simulated.
128 devices in a mesh: wave: 16 (over z, x), level: 8 (over y, core).
Axes of the slice: x: 4, y: 4, z: 4, core: 2. Of those that a mesh axis runs over, the one named last changes fastest.
Arguments:
- spec_in: float32 [640, 2, 16, 2, 1281], P('wave', None, 'level'), may hold values from -0.0034179688 to 0.0034179688
- legendre: float32 [640, 64, 1281], P('wave'), may hold values from -6 to 6
- gauss: float32 [64], replicated, may hold values from 0.3 to 3
- wave_map: int32 [640], replicated, may hold values from 0 to 639, each once
- band_map: int32 [128], replicated, may hold values from 0 to 127, each once
- row_len: int32 [64], replicated, may hold values from 20 to 5136, as said below
Outputs:
- grid_out: float32 [128, 2, 16, 5248], P(('wave', 'level'))
- spec_out: float32 [640, 5, 16, 2, 1281], P('wave', None, 'level')
Inputs may be any that keep to these rules, and one draw needn't show every extreme that they name: `wave_map`: each pair index appears once. `band_map`: each row appears once. `row_len`: each length is 20 + 4 j for distinct j of 0 to 1279; the rows of 20 and of 5136 points are always among them.
All inputs are finite; a program needn't handle non-finite values.
Results may differ from a plain program's by a relative error of at most 0.0003.
Values sent between devices are 32-bit elements; how exact they have to be, the bound alone decides.
A program may use at most 192 MiB of HBM per device.

v0:
```python
import math

import jax
import jax.numpy as jnp
from jax import lax
from jax.sharding import PartitionSpec as P

EXACT_DOT = lax.Precision.HIGHEST
FULL_TURN = 2.0 * math.pi
HALF_BLOCK = 128


def split_parity(array, half_len):
    lead = array.shape[:-1]
    extra = 2 * half_len - array.shape[-1]
    padded = jnp.pad(array, [(0, 0)] * len(lead) + [(0, extra)])
    paired = padded.reshape(lead + (half_len, 2))
    both = jnp.stack([paired[..., 0], paired[..., 1]])
    return both.reshape((2,) + lead + (half_len // HALF_BLOCK, HALF_BLOCK))


def pick_block(array, mixed):
    index = mixed[:, :, None, None, None]
    return jnp.take_along_axis(array, index, axis=3)[:, :, :, 0, :]


def row_angles(wave_ids, lon_ids, length):
    turns = wave_ids * lon_ids % length
    return turns.astype(jnp.float32) * (FULL_TURN / length.astype(jnp.float32))


def row_work(real_part, imag_part, length, wave_count, pad_len):
    field_count, level_count, _ = real_part.shape
    width = field_count * level_count
    wave_block = math.gcd(wave_count, 128)
    block_count = wave_count // wave_block
    lon_block = 128 * min(6, pad_len // 128)
    lon_total = (pad_len + lon_block - 1) // lon_block * lon_block
    highest = jnp.minimum(wave_count - 1, (length - 1) // 2)
    wave_ids = jnp.arange(wave_count, dtype=jnp.int32)
    weight = jnp.where(wave_ids == 0, 1.0, 2.0).astype(jnp.float32)
    slope_weight = weight * wave_ids.astype(jnp.float32) / wave_count
    real_rows = real_part.reshape(width, wave_count)
    imag_rows = imag_part.reshape(width, wave_count)
    on_cosine = jnp.concatenate([real_rows * weight, -imag_rows * slope_weight], axis=0)
    on_sine = jnp.concatenate([-imag_rows * weight, -real_rows * slope_weight], axis=0)
    lon_trips = (length + lon_block - 1) // lon_block
    wave_trips = highest // wave_block + 1

    def lon_step(lon_pos, carry):
        grid_rows, cos_sums, sin_sums = carry
        lon_ids = lon_pos * lon_block + jnp.arange(lon_block, dtype=jnp.int32)

        def forward_step(block_pos, state):
            partial_grid, tables = state
            block_ids = block_pos * wave_block + jnp.arange(wave_block, dtype=jnp.int32)
            angle = row_angles(block_ids[:, None], lon_ids[None, :], length)
            inside = ((lon_ids[None, :] < length) & (block_ids[:, None] <= highest)).astype(
                jnp.float32
            )
            stacked = jnp.concatenate([jnp.cos(angle) * inside, jnp.sin(angle) * inside], axis=0)
            start = block_pos * wave_block
            coeffs = jnp.concatenate(
                [
                    lax.dynamic_slice_in_dim(on_cosine, start, wave_block, 1),
                    lax.dynamic_slice_in_dim(on_sine, start, wave_block, 1),
                ],
                axis=1,
            )
            partial_grid = partial_grid + jnp.dot(
                coeffs, stacked, precision=EXACT_DOT, preferred_element_type=jnp.float32
            )
            tables = lax.dynamic_update_index_in_dim(tables, stacked, block_pos, 0)
            return (partial_grid, tables)

        start_state = (
            jnp.zeros((2 * width, lon_block), jnp.float32),
            jnp.zeros((block_count, 2 * wave_block, lon_block), jnp.float32),
        )
        block_grid, tables = lax.fori_loop(0, wave_trips, forward_step, start_state)
        values = block_grid.reshape(2, field_count, level_count, lon_block)
        field = values[0]
        slope = values[1]
        fluxes = jnp.concatenate(
            [
                field[0] * field[0],
                field[0] * field[1],
                field[1] * field[1],
                field[0] * slope[0],
                field[0] * slope[1],
            ],
            axis=0,
        )

        def backward_step(block_pos, sums):
            cos_part, sin_part = sums
            stacked = lax.dynamic_index_in_dim(tables, block_pos, 0, keepdims=False)
            product = jnp.einsum(
                "ck,mk->cm",
                fluxes,
                stacked,
                precision=EXACT_DOT,
                preferred_element_type=jnp.float32,
            )
            start = block_pos * wave_block
            cos_part = lax.dynamic_update_slice_in_dim(
                cos_part,
                lax.dynamic_slice_in_dim(cos_part, start, wave_block, 1) + product[:, :wave_block],
                start,
                1,
            )
            sin_part = lax.dynamic_update_slice_in_dim(
                sin_part,
                lax.dynamic_slice_in_dim(sin_part, start, wave_block, 1) + product[:, wave_block:],
                start,
                1,
            )
            return (cos_part, sin_part)

        cos_sums, sin_sums = lax.fori_loop(0, wave_trips, backward_step, (cos_sums, sin_sums))
        grid_rows = lax.dynamic_update_slice_in_dim(grid_rows, field, lon_pos * lon_block, 2)
        return (grid_rows, cos_sums, sin_sums)

    start_carry = (
        jnp.zeros((field_count, level_count, lon_total), jnp.float32),
        jnp.zeros((5 * level_count, wave_count), jnp.float32),
        jnp.zeros((5 * level_count, wave_count), jnp.float32),
    )
    grid_rows, cos_sums, sin_sums = lax.fori_loop(0, lon_trips, lon_step, start_carry)
    scale = length.astype(jnp.float32)
    back = jnp.stack([cos_sums / scale, -sin_sums / scale], axis=1).reshape(
        5, level_count, 2, wave_count
    )
    return (grid_rows[:, :, :pad_len], back)


def shards(spec_in, legendre, gauss, wave_map, band_map, row_len):
    wave_devices = lax.axis_size("wave")
    level_devices = lax.axis_size("level")
    wave_pos = lax.axis_index("wave")
    level_pos = lax.axis_index("level")
    local_pairs, _, level_share, _, pack_len = spec_in.shape
    wave_count = pack_len - 1
    lat_pairs = legendre.shape[1]
    row_count = 2 * lat_pairs
    lat_share = row_count // (wave_devices * level_devices)
    level_count = level_share * level_devices
    pad_len = (20 + 4 * (wave_count - 1) + 127) // 128 * 128
    slot_count = 2 * local_pairs
    own_pairs = lax.dynamic_slice_in_dim(wave_map, wave_pos * local_pairs, local_pairs)
    half_len = ((pack_len + 1) // 2 + HALF_BLOCK - 1) // HALF_BLOCK * HALF_BLOCK
    block_total = half_len // HALF_BLOCK
    boundary = wave_count - own_pairs
    limits = jnp.stack([(boundary + 1) // 2, boundary // 2])
    mixed = jnp.minimum(limits // HALF_BLOCK, block_total - 1)
    block_ids = jnp.arange(block_total, dtype=jnp.int32)
    whole_first = (
        ((block_ids + 1) * HALF_BLOCK <= limits[:, :, None]) & (block_ids != mixed[:, :, None])
    ).astype(jnp.float32)
    mixed_hot = (block_ids == mixed[:, :, None]).astype(jnp.float32)
    inner_ids = jnp.arange(HALF_BLOCK, dtype=jnp.int32)
    mixed_keep = (mixed[:, :, None] * HALF_BLOCK + inner_ids < limits[:, :, None]).astype(
        jnp.float32
    )
    parity_sign = (1 - 2 * (boundary % 2)).astype(jnp.float32)[:, None, None]
    leg_split = split_parity(legendre, half_len)
    leg_mixed = pick_block(leg_split, mixed)
    flat_in = spec_in.reshape(local_pairs, 4 * level_share, pack_len)
    coef_split = split_parity(flat_in, half_len)
    block_sums = jnp.einsum(
        "spcbk,sprbk->spbcr",
        coef_split,
        leg_split,
        precision=EXACT_DOT,
        preferred_element_type=jnp.float32,
    )
    total_sums = jnp.sum(block_sums, axis=2)
    first_sums = jnp.sum(block_sums * whole_first[:, :, :, None, None], axis=2)
    coef_mixed = pick_block(coef_split, mixed) * mixed_keep[:, :, None, :]
    first_sums = first_sums + jnp.einsum(
        "spck,sprk->spcr",
        coef_mixed,
        leg_mixed,
        precision=EXACT_DOT,
        preferred_element_type=jnp.float32,
    )
    second_sums = total_sums - first_sums
    values = jnp.stack(
        [
            first_sums[0] + first_sums[1],
            first_sums[0] - first_sums[1],
            second_sums[0] + second_sums[1],
            parity_sign * (second_sums[0] - second_sums[1]),
        ],
        axis=1,
    )
    values = values.reshape(local_pairs, 2, 2, 4 * level_share, lat_pairs).transpose(0, 1, 3, 2, 4)
    values = values.reshape(slot_count, 4 * level_share, row_count)
    values = jnp.take(values, band_map, axis=2)
    outgoing = values.reshape(
        slot_count, 4 * level_share, wave_devices, level_devices, lat_share
    ).transpose(2, 3, 0, 1, 4)
    joined = outgoing.reshape((wave_devices * level_devices,) + outgoing.shape[2:])
    arrived = lax.all_to_all(
        joined, ("wave", "level"), split_axis=0, concat_axis=0, tiled=True
    ).reshape(outgoing.shape)
    arrived = arrived.reshape(wave_devices, level_devices, slot_count, 2, level_share, 2, lat_share)
    arrived = arrived.transpose(6, 5, 3, 1, 4, 0, 2).reshape(
        lat_share, 2, 2, level_count, wave_count
    )
    wave_of_slot = jnp.stack([wave_map, wave_count - 1 - wave_map], axis=1).reshape(wave_count)
    slot_of_wave = (
        jnp.zeros((wave_count,), jnp.int32)
        .at[wave_of_slot]
        .set(jnp.arange(wave_count, dtype=jnp.int32))
    )
    spectra = jnp.take(arrived, slot_of_wave, axis=4)
    band_rows = lax.dynamic_slice_in_dim(
        band_map, (wave_pos * level_devices + level_pos) * lat_share, lat_share
    )
    own_lengths = jnp.take(row_len, band_rows % lat_pairs)
    grid_list, back_list = ([], [])
    grid_part, back_part = row_work(
        spectra[0, 0], spectra[0, 1], own_lengths[0], wave_count, pad_len
    )
    grid_list.append(grid_part)
    back_list.append(back_part)
    grid_out = jnp.stack(grid_list)
    back = jnp.stack(back_list)
    back = jnp.take(back, wave_of_slot, axis=4)
    back = back.reshape(lat_share, 5, level_devices, level_share, 2, wave_devices, slot_count)
    returning = back.transpose(5, 2, 0, 1, 3, 4, 6)
    joined_back = returning.reshape((wave_devices * level_devices,) + returning.shape[2:])
    returned = lax.all_to_all(
        joined_back, ("wave", "level"), split_axis=0, concat_axis=0, tiled=True
    ).reshape(returning.shape)
    returned = returned.reshape(row_count, 10 * level_share, slot_count)
    row_order = (
        jnp.zeros((row_count,), jnp.int32).at[band_map].set(jnp.arange(row_count, dtype=jnp.int32))
    )
    natural = jnp.take(returned, row_order, axis=0)
    weights = jnp.concatenate([gauss, gauss])
    natural = natural * weights[:, None, None]
    stacked = natural.reshape(2, lat_pairs, 10 * level_share, local_pairs, 2).transpose(
        3, 4, 0, 2, 1
    )
    stacked = stacked.reshape(local_pairs, 4, 10 * level_share, lat_pairs)
    first_rows = jnp.stack([stacked[:, 0] + stacked[:, 1], stacked[:, 0] - stacked[:, 1]])
    second_rows = jnp.stack(
        [stacked[:, 2] + parity_sign * stacked[:, 3], stacked[:, 2] - parity_sign * stacked[:, 3]]
    )
    chosen = jnp.where(
        whole_first[:, :, :, None, None] > 0.5, first_rows[:, :, None], second_rows[:, :, None]
    )
    out_blocks = jnp.einsum(
        "spbcr,sprbk->spcbk",
        chosen,
        leg_split,
        precision=EXACT_DOT,
        preferred_element_type=jnp.float32,
    )
    with_first = jnp.einsum(
        "spcr,sprk->spck",
        first_rows,
        leg_mixed,
        precision=EXACT_DOT,
        preferred_element_type=jnp.float32,
    )
    with_second = jnp.einsum(
        "spcr,sprk->spck",
        second_rows,
        leg_mixed,
        precision=EXACT_DOT,
        preferred_element_type=jnp.float32,
    )
    mixed_values = jnp.where(mixed_keep[:, :, None, :] > 0.5, with_first, with_second)
    hot = mixed_hot[:, :, None, :, None]
    out_blocks = out_blocks * (1.0 - hot) + hot * mixed_values[:, :, :, None, :]
    merged = out_blocks.reshape(2, local_pairs, 10 * level_share, half_len).transpose(1, 2, 3, 0)
    merged = merged.reshape(local_pairs, 10 * level_share, 2 * half_len)[:, :, :pack_len]
    spec_out = merged.reshape(local_pairs, 5, level_share, 2, pack_len)
    return (grid_out, spec_out)


def solution(mesh):
    in_specs = (P("wave", None, "level", None, None), P("wave", None, None), P(), P(), P(), P())
    out_specs = (P(("wave", "level"), None, None, None), P("wave", None, "level", None, None))
    return jax.shard_map(shards, mesh=mesh, in_specs=in_specs, out_specs=out_specs, check_vma=False)
```

profile of v0, /device:TPU:1, one launch (start us, length us, event | category | flops | bytes accessed | tf_op | source)
XLA Modules:
  0.0 1047.0 jit_solution(13362481163541033413)
XLA Ops:
  3.5 20.6 %copy.175 = f32[40,64,1281]{1,0,2:T(8,128)} copy(f32[40,64,1281]{2,1,0:T(8,128)} %param.13) | data formatting | bytes 26234880
  24.1 22.0 %pad.9.clone = f32[40,64,1536]{1,0,2:T(8,128)} pad(f32[40,64,1281]{1,0,2:T(8,128)} %copy.175, f32[]{:T(128)} %constant.281.clone.1), padding=0_0x0_0x0_255 | pad | bytes 28846084 | tf_op jit(solution)/shard_map/jit(_pad)/pad | solution.py:16
  46.2 21.0 %fusion.77 = (f32[40,64,768,1]{1,0,3,2:T(8,128)}, f32[40,64,768,1]{1,0,3,2:T(8,128)}) fusion(f32[40,64,768,2]{1,0,3,2:T(8,128)} %bitcast.121), kind=kLoop, calls=%fused_computation.184 | loop fusion | bytes 31457280 | tf_op jit(solution)/shard_map/slice | solution.py:18
  67.2 14.8 %copy.141 = f32[1,40,64,6,128]{4,2,3,1,0:T(8,128)} copy(f32[1,40,64,6,128]{2,1,4,3,0:T(8,128)} %bitcast.127) | data formatting | bytes 15728640 | tf_op jit(solution)/shard_map/stack | solution.py:18
  81.9 14.9 %copy.142 = f32[1,40,64,6,128]{4,2,3,1,0:T(8,128)} copy(f32[1,40,64,6,128]{2,1,4,3,0:T(8,128)} %bitcast.126) | data formatting | bytes 15728640 | tf_op jit(solution)/shard_map/stack | solution.py:18
  96.8 6.2 copy.166
  113.2 14.6 %pad_maximum_fusion.2 = f32[2,40,64,6,128]{4,2,3,1,0:T(8,128)} fusion(f32[1,40,64,6,128]{4,2,3,1,0:T(8,128)} %copy.142, f32[1,40,64,6,128]{4,2,3,1,0:T(8,128)} %copy.141), kind=kLoop, calls=%fused_computation.46 | loop fusion | flops 3932160 | bytes 31457280 | tf_op jit(solution)/shard_map/stack | solution.py:18
  129.2 28.3 %multiply_reduce_fusion = (f32[2,40,8,64]{3,2,1,0:T(8,128)S(1)}, f32[2,40,8,64]{3,2,1,0:T(8,128)}) fusion(f32[2,40,6]{2,1,0:T(8,128)S(1)} %get-tuple-element.461, f32[1,40,64,6,128]{4,2,3,1,0:T(8,128)} %copy.142, f32[1,40,64,6,128]{4,2,3,1,0:T(8,128)} %copy.141, f32[1,40,8,6,128]{4,2,3,1,0:T(8,128)S(1)} %bitcast.140, f32[1,40,8,6,128]{4,2,3,1,0:T(8,128)S(1)} %bitcast.138), kind=kOutput, calls=%fused_computation.61 | convolution fusion | flops 382566400 | bytes 18024320 | tf_op jit(solution)/shard_map/spcbk,sprbk->spbcr/dot_general | solution.py:170
  157.8 6.6 gather_fusion.5
  176.8 11.5 %all-to-all-start = ((f32[128,80,8,1]{1,2,3,0:T(8,128)}), f32[128,80,8,1]{1,2,3,0:T(8,128)S(1)}, u32[]{:S(2)}, u32[]{:S(2)}) async-start(f32[128,80,8,1]{1,2,3,0:T(8,128)} %copy.147), calls=%async_computation | async-start | bytes 1048576 | tf_op jit(solution)/shard_map/all_to_all | solution.py:204
  203.5 5.8 gather_fusion.1
  212.5 19.9 %while.58 = (s32[]{:T(128)}, f32[2,16,5376]{2,1,0:T(8,128)S(1)}, f32[80,1280]{1,0:T(8,128)S(1)}, f32[80,1280]{1,0:T(8,128)S(1)}, s32[]{:T(128)}, /*index=5*/s32[...) while((s32[]{:T(128)}, f32[2,16,5376]{2,1,0:T(8,128)S(1)}, ...), condition=%wide.region_8.9_spmd, body=%wide.region_3.8_spmd.sunk | while | flops 341559936 | bytes 14198522 | solution.py:129
  216.3 7.0 while.59
  240.3 6.7 copy.154
  247.0 9.9 maximum_bitcast_fusion
  256.9 19.0 %gather_fusion.2 = f32[1280,5,16,2]{2,3,1,0:T(2,128)} fusion(f32[5,16,2,1280]{1,2,3,0:T(2,128)} %maximum_bitcast_fusion, s32[2048]{0:T(1024)S(1)} %pad_clamp_fusion), kind=kCustom, calls=%fused_computation.2 | custom fusion | bytes 1643520 | tf_op jit(solution)/shard_map/jit(_take)/gather | solution.py:230
  276.0 6.8 copy.155
  286.6 655.6 %all-to-all-start.1 = ((f32[128,1,5,2,2,80]{5,4,3,2,1,0:T(2,128)}), f32[128,1,5,2,2,80]{5,4,3,2,1,0:T(2,128)S(1)}, u32[]{:S(2)}, u32[]{:S(2)}) async-start(f32[128,1,5,2,2,80]{5,4,3,2,1,0:T(2,128)} %copy.157), calls=%async_computation.1 | async-start | bytes 2621440 | tf_op jit(solution)/shard_map/all_to_all | solution.py:234
  943.1 20.7 %all-to-all-done.1 = f32[128,1,5,2,2,80]{5,4,3,2,1,0:T(2,128)S(1)} async-done(((f32[128,1,5,2,2,80]{5,4,3,2,1,0:T(2,128)}), f32[128,1,5,2,2,80]{5,4,3,2,1,0:T(2,128)S(1)}, u32[]{:S(2)}, u32[]{:S(2)}) %all-to-all-start.1) | async-done | bytes 819232 | tf_op jit(solution)/shard_map/all_to_all | solution.py:234
  978.5 17.0 %bitcast_add_fusion = f32[2,40,20,6,128]{4,2,3,1,0:T(8,128)S(1)} fusion(f32[2,40,20,128]{3,2,1,0:T(8,128)} %fusion.30, f32[2,40,6]{2,1,0:T(8,128)S(1)} %get-tuple-element.464, f32[2,40,6]{2,1,0:T(8,128)S(1)} %broadcast_subtract_fusion, f32[2,40,20,64]{3,2,1,0:T(8,128)S(1)} %pad_maximum_fusion.5, f32[2,40,20,64]{3,2,1,0:T(8,128)S(1)} %pad_maximum_fusion.4, ...), kind=kOutput, calls=%fused_computation.48 | convolution fusion | flops 951951360 | bytes 22286560 | tf_op jit(solution)/shard_map/spbcr,sprbk->spcbk/dot_general | solution.py:255
  999.6 7.0 reshape.712
  1006.5 18.5 %copy.163 = f32[40,20,768,2]{0,3,2,1:T(2,128)} copy(f32[40,20,768,2]{2,0,1,3:T(8,128)} %bitcast.135) | data formatting | bytes 9830400 | tf_op jit(solution)/shard_map/transpose | solution.py:279
  1025.0 10.3 slice.158
  1035.4 11.2 %copy.165 = f32[40,5,2,2,1281]{4,3,2,1,0:T(2,128)} copy(f32[40,5,2,2,1281]{0,4,3,2,1:T(8,128)} %bitcast.129) | data formatting | bytes 8198400
  (150 shorter events, 88.3 us)
Async XLA Ops:
  81.9 14.9 %copy-start.7 = (f32[40,2,2,2,1281]{4,3,2,1,0:T(2,128)S(1)}, f32[40,2,2,2,1281]{4,3,2,1,0:T(2,128)}, u32[]{:S(2)}) copy-start(f32[40,2,2,2,1281]{4,3,2,1,0:T(2,128)} %param.12) | copy-start | bytes 4919044
  113.2 14.7 %copy-start.2 = (f32[40,8,768,1]{2,1,0,3:T(8,128)S(1)}, f32[40,8,768,1]{2,1,0,3:T(8,128)}, u32[]{:S(2)}) copy-start(f32[40,8,768,1]{2,1,0,3:T(8,128)} %copy.136) | copy-start | bytes 2949124
  113.2 14.6 %copy-start.3 = (f32[40,8,768,1]{2,1,0,3:T(8,128)S(1)}, f32[40,8,768,1]{2,1,0,3:T(8,128)}, u32[]{:S(2)}) copy-start(f32[40,8,768,1]{2,1,0,3:T(8,128)} %copy.137) | copy-start | bytes 2949124
  164.4 9.7 copy-start
  173.3 15.1 %copy-start.8 = (s32[640]{0:T(1024)S(1)}, s32[640]{0:T(1024)}, u32[]{:S(2)}) copy-start(s32[640]{0:T(1024)} %param.15) | copy-start | bytes 7684
  173.4 20.7 %copy-start.9 = (s32[128]{0:T(128)S(1)}, s32[128]{0:T(128)}, u32[]{:S(2)}) copy-start(s32[128]{0:T(128)} %param.16) | copy-start | bytes 1540
  173.4 23.3 %copy-start.10 = (s32[64]{0:T(128)S(1)}, s32[64]{0:T(128)}, u32[]{:S(2)}) copy-start(s32[64]{0:T(128)} %param.17) | copy-start | bytes 772
  173.4 26.0 %copy-start.11 = (f32[64]{0:T(128)S(1)}, f32[64]{0:T(128)}, u32[]{:S(2)}) copy-start(f32[64]{0:T(128)} %param.14) | copy-start | bytes 772
  176.8 25.0 %all-to-all-start = ((f32[128,80,8,1]{1,2,3,0:T(8,128)}), f32[128,80,8,1]{1,2,3,0:T(8,128)S(1)}, u32[]{:S(2)}, u32[]{:S(2)}) async-start(f32[128,80,8,1]{1,2,3,0:T(8,128)} %copy.147), calls=%async_computation | async-start | bytes 1048576 | tf_op jit(solution)/shard_map/all_to_all | solution.py:204
  232.4 0.9 copy-start.4
  232.5 1.1 copy-start.5
  283.8 658.5 %copy-start.6 = (f32[2,16,5376]{2,1,0:T(8,128)S(1)}, f32[2,16,5376]{2,1,0:T(8,128)}, u32[]{:S(2)}) copy-start(f32[2,16,5376]{2,1,0:T(8,128)} %copy-done.5) | copy-start | bytes 2064388
  286.6 677.2 %all-to-all-start.1 = ((f32[128,1,5,2,2,80]{5,4,3,2,1,0:T(2,128)}), f32[128,1,5,2,2,80]{5,4,3,2,1,0:T(2,128)S(1)}, u32[]{:S(2)}, u32[]{:S(2)}) async-start(f32[128,1,5,2,2,80]{5,4,3,2,1,0:T(2,128)} %copy.157), calls=%async_computation.1 | async-start | bytes 2621440 | tf_op jit(solution)/shard_map/all_to_all | solution.py:234
  969.6 8.9 slice-start.2
  970.6 2.1 copy-start.1
  970.6 7.9 slice-start
  971.8 6.7 slice-start.3
  972.6 5.9 slice-start.1
where the time goes:
time: 1060 us; the launch traced here: 1050 us
  starting transfers between devices  667 us (63%)
  local copies, waits for them, and re-layouts  246 us (23%)
  matrix products  59 us (6%)
  other arithmetic  40.3 us (4%)
  waiting for transfers between devices  22.8 us (2%)
    all_to_all x1, starting transfers between devices, shards(): lax.all_to_all(joined_back, ('wave', 'level'), split_axis=0, concat_axis=...  656 us
    unnamed x36, local copies, waits for them, and re-layouts  32.9 us
    another operation x2, local copies, waits for them, and re-layouts, split_parity(): both = jnp.stack([paired[..., 0], paired[..., 1]])  29.7 us
    dot_general x1, matrix products, shards(): jnp.einsum('spcbk,sprbk->spbcr', coef_split, leg_split, precision=EXACT_D...  28.3 us
    slice x4, local copies, waits for them, and re-layouts, split_parity(): both = jnp.stack([paired[..., 0], paired[..., 1]])  28.1 us
    gather x3, local copies, waits for them, and re-layouts, shards(): back = jnp.take(back, wave_of_slot, axis=4)  26.7 us
    pad x2, local copies, waits for them, and re-layouts, split_parity(): padded = jnp.pad(array, [(0, 0)] * len(lead) + [(0, extra)])  24.9 us
  transfers between devices with their start and end apart: 2, of which 2 were waited for; matrix products, arithmetic and copies ran while one was open for 1% of the time, Pallas kernels for 0%

commit v1 on v0

v1 whole, which is shorter than its diff:
```python
import functools
import math

import jax
import jax.numpy as jnp
from jax import lax
from jax.experimental import pallas as pl
from jax.experimental.pallas import tpu as pltpu
from jax.sharding import PartitionSpec as P

F32 = jnp.float32
BF16 = jnp.bfloat16
LANES = 128
MIB = 1 << 20
SIN_TERMS = [(-1.0) ** i / math.factorial(2 * i + 1) for i in range(6)]
COS_TERMS = [(-1.0) ** i / math.factorial(2 * i) for i in range(7)]
NT = (((1,), (1,)), ((), ()))
NN = (((1,), (0,)), ((), ()))


def dot(a, b, dims):
    return lax.dot_general(a, b, dims, preferred_element_type=F32)


def split(x):
    high = x.astype(BF16)
    return high, (x - high.astype(F32)).astype(BF16)


def horner(terms, x):
    total = jnp.full_like(x, terms[-1])
    for term in reversed(terms[:-1]):
        total = total * x + term
    return total


def turn_trig(steps, length, inverse):
    left = steps - jnp.floor(steps * inverse + 0.5) * length
    half = left * (inverse * math.pi)
    square = half * half
    sine = half * horner(SIN_TERMS, square)
    cosine = horner(COS_TERMS, square)
    return 1.0 - 2.0 * sine * sine, 2.0 * sine * cosine


def inverse_kernel(group, wave_ref, band_ref, spec_ref, leg_ref, out_ref, flat, sums, rows):
    step = pl.program_id(0)
    slots = sums.shape[0] // 32
    pack = leg_ref.shape[2]
    wave_pos = lax.axis_index("wave")
    position = lax.broadcasted_iota(jnp.int32, (8, pack), 1)
    for g in range(group):
        slot = step * group + g
        first_wave = wave_ref[wave_pos * slots + slot]
        boundary = (pack - 1) - first_wave
        for pair in range(4):
            flat[2 * pair : 2 * pair + 2, :] = spec_ref[g, pair // 2, pair % 2]
        x = flat[...]
        in_first = position < boundary
        parity = jnp.where(in_first, position, position + boundary) & 1
        in_even = in_first == ((first_wave & 1) == 0)
        high = x.astype(BF16).astype(F32)
        parts = []
        for part in (high, x - high):
            signed = jnp.where(parity == 0, part, -part)
            for kept in (in_even, jnp.logical_not(in_even)):
                parts += [jnp.where(kept, part, 0.0), jnp.where(kept, signed, 0.0)]
        left = jnp.concatenate(parts, axis=0).astype(BF16)
        right = jnp.concatenate(split(leg_ref[g]), axis=0)
        both = dot(left, right, NT)
        both = both[:32] + both[32:]
        sums[pl.ds(pl.multiple_of(slot * 32, 32), 32), :] = both + pltpu.roll(both, 64, 1)

    @pl.when(step == pl.num_programs(0) - 1)
    def _():
        north = lax.broadcasted_iota(jnp.int32, (slots, LANES), 1) < 64
        for c in range(8):
            v = [sums[pl.ds(8 * i + c, slots, stride=32), :] for i in range(4)]
            block = jnp.concatenate(
                [
                    jnp.where(north, v[0], v[1]),
                    jnp.where(north, v[2], v[3]),
                    jnp.zeros((LANES - 2 * slots, LANES), F32),
                ],
                axis=0,
            )
            rows[pl.ds(c, LANES, stride=8), :] = block.T

        @pl.loop(0, out_ref.shape[0], unroll=8)
        def _(i):
            out_ref[i] = rows[pl.ds(pl.multiple_of(band_ref[i] * 8, 8), 8), :]


def row_kernel(
    band_ref, len_ref, gauss_ref, row_ref, col_ref, in_ref, grid_ref, out_ref,
    sorted_x, even_x, odd_x, even_l, odd_l, even_hi, even_lo, odd_hi, odd_lo, segs, even_f, odd_f, acc, back, packed,
):
    here = lax.axis_index("wave") * lax.axis_size("level") + lax.axis_index("level")
    row = band_ref[here] & 63
    length = len_ref[row]
    quarter = lax.shift_right_logical(length, 2)
    wave_top = 2 * row_ref.shape[1] - 1
    length_f = jnp.full((1, LANES), length.astype(F32))
    inverse = 1.0 / length_f
    half_waves = row_ref.shape[1]
    blocks = half_waves // LANES
    devices = in_ref.shape[0]
    share = half_waves // devices
    tiles = even_hi.shape[1] // LANES
    lane = lax.broadcasted_iota(jnp.int32, (1, LANES), 1)

    @pl.loop(0, half_waves // 32)
    def _(group):
        block, inner = group // 4, group % 4
        at_cos = pl.multiple_of(block * 256 + inner * 32, 32)
        at_sin = pl.multiple_of(block * 256 + LANES + inner * 32, 32)
        evens = jnp.broadcast_to(col_ref[pl.ds(pl.multiple_of(group * 32, 32), 32), :], (32, LANES))
        for waves, table_hi, table_lo in ((evens, even_hi, even_lo), (wave_top - evens, odd_hi, odd_lo)):
            cosine, sine = turn_trig(waves * lane.astype(F32), length_f, inverse)
            turn_cos, turn_sin = turn_trig(waves * float(LANES), length_f, inverse)
            for tile in range(tiles):
                at = slice(tile * LANES, (tile + 1) * LANES)
                high, low = split(cosine)
                table_hi[pl.ds(at_cos, 32), at] = high
                table_lo[pl.ds(at_cos, 32), at] = low
                high, low = split(sine)
                table_hi[pl.ds(at_sin, 32), at] = high
                table_lo[pl.ds(at_sin, 32), at] = low
                if tile < tiles - 1:
                    cosine, sine = (
                        cosine * turn_cos - sine * turn_sin,
                        sine * turn_cos + cosine * turn_sin,
                    )

    for dev in range(devices):
        for c in range(8):
            f, lv, part = c // 4, c // 2 % 2, c % 2
            piece = in_ref[dev, pl.ds(c, 8, stride=8), :]
            sorted_x[dev % 4, pl.ds(32 * part + 16 * f + lv, 8, stride=2), :] = piece
        at = slice(dev * share, (dev + 1) * share)
        even_x[:, at] = sorted_x[dev % 4, :, :share]
        odd_x[:, at] = sorted_x[dev % 4, :, share : 2 * share]

    highest = jnp.minimum(wave_top, lax.shift_right_logical(length - 1, 1))
    for block in range(blocks):
        at = slice(block * LANES, (block + 1) * LANES)
        evens = row_ref[:, at]
        for odd, x_ref, l_ref in ((False, even_x, even_l), (True, odd_x, odd_l)):
            wave = wave_top - evens if odd else evens
            kept = (wave <= highest).astype(F32)
            weight = jnp.where(wave == 0, 1.0, 2.0) * kept
            slope_weight = weight * wave.astype(F32) / (wave_top + 1.0)
            real, imag = x_ref[0:32, at], x_ref[32:64, at]
            a = jnp.concatenate([real * weight, -imag * slope_weight], axis=0)
            b = jnp.concatenate([imag * weight, real * slope_weight], axis=0)
            flip = (1 - (wave & 2)).astype(F32)
            if odd:
                on_cos = jnp.concatenate([a, flip * b], axis=0)
                on_sin = jnp.concatenate([-b, flip * a], axis=0)
            else:
                on_cos = jnp.concatenate([a, flip * a], axis=0)
                on_sin = jnp.concatenate([-b, -flip * b], axis=0)
            for offset, value in ((0, on_cos), (LANES, on_sin)):
                to = slice(block * 256 + offset, block * 256 + offset + LANES)
                high, low = split(value)
                l_ref[0:128, to] = high
                l_ref[128:256, to] = low

    start = 0
    while start < tiles * LANES:
        width = min(256, tiles * LANES - start)
        at = slice(start, start + width)
        start += width
        halves = []
        for l_ref, table_hi, table_lo in ((even_l, even_hi, even_lo), (odd_l, odd_hi, odd_lo)):
            whole = dot(l_ref[...], table_hi[:, at], NN)
            halves.append(whole[:128] + whole[128:] + dot(l_ref[0:128, :], table_lo[:, at], NN))
        inside = (at.start + lax.broadcasted_iota(jnp.int32, (1, width), 1)) < quarter
        even, odd = (jnp.where(inside, half, 0.0) for half in halves)
        quarters = [even[:64] + odd[:64], even[64:] - odd[64:], even[:64] - odd[:64], even[64:] + odd[64:]]
        fluxes = []
        for i, values in enumerate(quarters):
            segs[i, :, at] = values[:32]
            u, v, su, sv = (values[16 * n : 16 * n + 16] for n in range(4))
            fluxes.append(jnp.concatenate([u * u, u * v, v * v, u * su, u * sv], axis=0))
        for f_ref, sign in ((even_f, 1.0), (odd_f, -1.0)):
            for n in range(2):
                value = fluxes[n] + fluxes[n + 2] if sign > 0 else fluxes[n] - fluxes[n + 2]
                high, low = split(value)
                f_ref[80 * n : 80 * n + 80, at] = high
                f_ref[160 + 80 * n : 240 + 80 * n, at] = low

    acc[...] = jnp.zeros_like(acc)
    for i in range(4):
        begin = i * quarter
        shift = begin & (LANES - 1)
        base = lax.shift_right_logical(begin, 7)
        before = jnp.zeros((32, LANES), F32)
        for tile in range(tiles + 1):
            if tile < tiles:
                rolled = pltpu.roll(segs[i, :, tile * LANES : (tile + 1) * LANES], shift, 1)
            else:
                rolled = jnp.zeros((32, LANES), F32)
            at = pl.ds(pl.multiple_of((base + tile) * LANES, LANES), LANES)
            acc[:, at] += jnp.where(lane < shift, before, rolled)
            before = rolled
    pad_len = grid_ref.shape[3]
    for f in range(2):
        grid_ref[0, f] = acc[16 * f : 16 * f + 16, :pad_len]

    scale = gauss_ref[row] * inverse
    for block in range(blocks):
        at = slice(block * LANES, (block + 1) * LANES)
        rows = slice(block * 256, (block + 1) * 256)
        evens = row_ref[:, at]
        for odd, f_ref, table_hi, table_lo in ((0, even_f, even_hi, even_lo), (1, odd_f, odd_hi, odd_lo)):
            whole = dot(f_ref[...], table_hi[rows, :], NT)
            total = whole[:160] + whole[160:] + dot(f_ref[0:160, :], table_lo[rows, :], NT)
            wave = wave_top - evens if odd else evens
            kept = jnp.where(wave <= highest, scale, 0.0)
            flip = (1 - (wave & 2)).astype(F32)
            first_cos, first_sin = total[:80, :LANES], total[:80, LANES:]
            second_cos, second_sin = total[80:, :LANES] * flip, total[80:, LANES:] * flip
            if odd:
                back[2, :, at] = (first_cos - second_sin) * kept
                back[3, :, at] = -(first_sin + second_cos) * kept
            else:
                back[0, :, at] = (first_cos + second_cos) * kept
                back[1, :, at] = -(first_sin + second_sin) * kept

    for dev in range(devices):
        at = slice(dev * share, (dev + 1) * share)
        for part in range(2):
            even, odd = back[part, :, at], back[2 + part, :, at]
            packed[part, :, 0:share] = even[:64]
            packed[part, :, share : 2 * share] = odd[:64]
            packed[part, 0:16, 2 * share : 3 * share] = even[64:]
            packed[part, 16:32, 2 * share : 3 * share] = odd[64:]
            for n in range(8):
                out_ref[dev, pl.ds(2 * n + part, 8, stride=16), :] = packed[
                    part, pl.ds(n // 2 * 16 + n % 2, 8, stride=2), :
                ]


def direct_kernel(group, wave_ref, band_ref, in_ref, leg_ref, out_ref, natural, turned):
    step = pl.program_id(0)
    pack = leg_ref.shape[2]
    slots = pl.num_programs(0) * group
    wave_pos = lax.axis_index("wave")

    @pl.when(step == 0)
    def _():
        @pl.loop(0, in_ref.shape[0], unroll=8)
        def _(i):
            natural[pl.ds(pl.multiple_of(band_ref[i] * 16, 16), 16), :] = in_ref[i]

        for n in range(16):
            turned[pl.ds(n, LANES, stride=16), :] = natural[pl.ds(n, LANES, stride=16), :].T

    position = lax.broadcasted_iota(jnp.int32, (1, pack), 1)
    south = lax.broadcasted_iota(jnp.int32, (1, LANES), 1) >= 64
    for g in range(group):
        slot = step * group + g
        first_wave = wave_ref[wave_pos * slots + slot]
        boundary = (pack - 1) - first_wave

        def of_lane(extra, count):
            return turned[pl.ds(pl.multiple_of((slot + extra) * 16, 16), count), :]

        x = jnp.concatenate([of_lane(0, 16), of_lane(slots, 16), of_lane(2 * slots, 8)], axis=0)
        other = pltpu.roll(x, 64, 1)
        difference = x - other
        y = jnp.concatenate([x + other, jnp.where(south, -difference, difference)], axis=0)
        left = jnp.concatenate(split(y), axis=0)
        right = jnp.concatenate(split(leg_ref[g]), axis=0)
        both = dot(left, right, NN)
        both = both[:80] + both[80:]
        in_first = position < boundary
        parity = jnp.where(in_first, position, position + boundary) & 1
        in_even = in_first == ((first_wave & 1) == 0)
        chosen = jnp.where(parity == 0, both[:40], both[40:])
        main = jnp.where(in_even, chosen[:16], chosen[16:32])
        last = jnp.where(in_even, chosen[32:36], chosen[36:40])
        for n in range(8):
            out_ref[g, n // 2, n % 2] = main[2 * n : 2 * n + 2]
        for n in range(2):
            out_ref[g, 4, n] = last[2 * n : 2 * n + 2]


def shards(spec_in, legendre, gauss, wave_map, band_map, row_len):
    axes = ("wave", "level")
    wave_devices = lax.axis_size("wave")
    devices = wave_devices * lax.axis_size("level")
    slots, _, _, _, pack = spec_in.shape
    waves = pack - 1
    lat_pairs = legendre.shape[1]
    pad_len = (20 + 4 * (waves - 1) + 127) // 128 * 128
    table_len = (pad_len // 4 + 127) // 128 * 128
    smem = pl.BlockSpec(memory_space=pltpu.SMEM)
    vmem = pl.BlockSpec(memory_space=pltpu.VMEM)
    group = 4

    outgoing = pl.pallas_call(
        functools.partial(inverse_kernel, group),
        out_shape=jax.ShapeDtypeStruct((devices, 8, LANES), F32),
        grid=(slots // group,),
        in_specs=[
            smem,
            smem,
            pl.BlockSpec((group, 2, 2, 2, pack), lambda s: (s, 0, 0, 0, 0)),
            pl.BlockSpec((group, lat_pairs, pack), lambda s: (s, 0, 0)),
        ],
        out_specs=pl.BlockSpec((devices, 8, LANES), lambda s: (0, 0, 0)),
        scratch_shapes=[
            pltpu.VMEM((8, pack), F32),
            pltpu.VMEM((slots * 32, LANES), F32),
            pltpu.VMEM((LANES * 8, LANES), F32),
        ],
        compiler_params=pltpu.CompilerParams(vmem_limit_bytes=32 * MIB),
        name="inverse",
    )(wave_map, band_map, spec_in, legendre)

    arrived = lax.all_to_all(outgoing, axes, split_axis=0, concat_axis=0, tiled=True)
    arrived = arrived.reshape(wave_devices, 64, LANES)
    evens = jnp.where(wave_map % 2 == 0, wave_map, waves - 1 - wave_map)
    grid_out, returning = pl.pallas_call(
        row_kernel,
        out_shape=(
            jax.ShapeDtypeStruct((1, 2, 16, pad_len), F32),
            jax.ShapeDtypeStruct((wave_devices, 128, LANES), F32),
        ),
        in_specs=[smem, smem, smem, vmem, vmem, vmem],
        out_specs=(vmem, vmem),
        scratch_shapes=[
            pltpu.VMEM((4, 64, LANES), F32),
            pltpu.VMEM((64, waves // 2), F32),
            pltpu.VMEM((64, waves // 2), F32),
            pltpu.VMEM((256, waves), BF16),
            pltpu.VMEM((256, waves), BF16),
            pltpu.VMEM((waves, table_len), BF16),
            pltpu.VMEM((waves, table_len), BF16),
            pltpu.VMEM((waves, table_len), BF16),
            pltpu.VMEM((waves, table_len), BF16),
            pltpu.VMEM((4, 32, table_len), F32),
            pltpu.VMEM((320, table_len), BF16),
            pltpu.VMEM((320, table_len), BF16),
            pltpu.VMEM((32, 4 * table_len), F32),
            pltpu.VMEM((4, 80, waves // 2), F32),
            pltpu.VMEM((2, 64, LANES), F32),
        ],
        compiler_params=pltpu.CompilerParams(vmem_limit_bytes=48 * MIB),
        name="rows",
    )(band_map, row_len, gauss, evens[None, :], evens[:, None].astype(F32), arrived)

    returning = returning.reshape(devices, 16, LANES)
    returned = lax.all_to_all(returning, axes, split_axis=0, concat_axis=0, tiled=True)
    spec_out = pl.pallas_call(
        functools.partial(direct_kernel, group),
        out_shape=jax.ShapeDtypeStruct((slots, 5, 2, 2, pack), F32),
        grid=(slots // group,),
        in_specs=[
            smem,
            smem,
            pl.BlockSpec((devices, 16, LANES), lambda s: (0, 0, 0)),
            pl.BlockSpec((group, lat_pairs, pack), lambda s: (s, 0, 0)),
        ],
        out_specs=pl.BlockSpec((group, 5, 2, 2, pack), lambda s: (s, 0, 0, 0, 0)),
        scratch_shapes=[
            pltpu.VMEM((LANES * 16, LANES), F32),
            pltpu.VMEM((LANES * 16, LANES), F32),
        ],
        compiler_params=pltpu.CompilerParams(vmem_limit_bytes=32 * MIB),
        name="direct",
    )(wave_map, band_map, returned, legendre)
    return (grid_out, spec_out)


def solution(mesh):
    in_specs = (P("wave", None, "level", None, None), P("wave", None, None), P(), P(), P(), P())
    out_specs = (P(("wave", "level"), None, None, None), P("wave", None, "level", None, None))
    return jax.shard_map(shards, mesh=mesh, in_specs=in_specs, out_specs=out_specs, check_vma=False)
```

time: 1060 us -> 97.7 us (0.09); the launches traced: 1050 us -> 97.3 us
  starting transfers between devices: 667 us -> 11.5 us
  local copies, waits for them, and re-layouts: 246 us -> 13.2 us
  matrix products: 59 us -> 0 us
  other arithmetic: 40.3 us -> 0.01 us
  Pallas kernels: 0 us -> 35.3 us
  blocking collectives: 0 us -> 23.3 us
    all_to_all x2 -> x1, starting transfers between devices: 667 us -> 11.5 us  [shards(): lax.all_to_all(outgoing, axes, split_axis=0, concat_axis=0, tiled=True)]
    dot_general x7 -> x0, matrix products: 59 us -> none  [the longest x1 28.3 us: shards(): jnp.einsum('spcbk,sprbk->spbcr', coef_split, leg_split, precision=EXACT_D...]
    gather x13 -> x0, local copies, waits for them, and re-layouts: 51.3 us -> none  [the longest x3 26.7 us: shards(): back = jnp.take(back, wave_of_slot, axis=4)]
    another operation x13 -> x0, local copies, waits for them, and re-layouts: 46.7 us -> none  [the longest x2 29.7 us: split_parity(): both = jnp.stack([paired[..., 0], paired[..., 1]])]
    slice x6 -> x0, local copies, waits for them, and re-layouts: 38.5 us -> none  [the longest x4 28.1 us: split_parity(): both = jnp.stack([paired[..., 0], paired[..., 1]])]
    pallas_call x0 -> x3, Pallas kernels: none -> 35.3 us  [the longest x1 16.2 us: shards(): pl.pallas_call(row_kernel, out_shape=(jax.ShapeDtypeStruct((1, 2, 16, pad...]
    another operation x7 -> x0, other arithmetic: 26.1 us -> none  [the longest x2 16 us: split_parity(): both = jnp.stack([paired[..., 0], paired[..., 1]])]
    pad x2 -> x0, local copies, waits for them, and re-layouts: 24.9 us -> none  [split_parity(): padded = jnp.pad(array, [(0, 0)] * len(lead) + [(0, extra)])]
  transfers between devices with their start and end apart: 2 -> 1, of which waited for: 2 -> 1; matrix products, arithmetic and copies ran while one was open for 1% -> 0% of each run, Pallas kernels for 0% -> 0%
where the time goes in v1:
time: 97.7 us; the launch traced here: 97.3 us
  Pallas kernels  35.3 us (36%)
  blocking collectives  23.3 us (24%)
  waiting for transfers between devices  13.3 us (14%)
  local copies, waits for them, and re-layouts  13.2 us (14%)
  starting transfers between devices  11.5 us (12%)
    all_to_all x1, blocking collectives, shards(): lax.all_to_all(returning, axes, split_axis=0, concat_axis=0, tiled=True)  23.3 us
    pallas_call x1, Pallas kernels, shards(): pl.pallas_call(row_kernel, out_shape=(jax.ShapeDtypeStruct((1, 2, 16, pad...  16.2 us
    all_to_all x1, waiting for transfers between devices, shards(): lax.all_to_all(outgoing, axes, split_axis=0, concat_axis=0, tiled=True)  13.3 us
    unnamed x18, local copies, waits for them, and re-layouts  13 us
    all_to_all x1, starting transfers between devices, shards(): lax.all_to_all(outgoing, axes, split_axis=0, concat_axis=0, tiled=True)  11.5 us
    pallas_call x1, Pallas kernels, shards(): pl.pallas_call(functools.partial(inverse_kernel, group), out_shape=jax.Sh...  9.73 us
    pallas_call x1, Pallas kernels, shards(): pl.pallas_call(functools.partial(direct_kernel, group), out_shape=jax.Sha...  9.43 us
  transfers between devices with their start and end apart: 1, of which 1 were waited for; matrix products, arithmetic and copies ran while one was open for 0% of the time, Pallas kernels for 0%

profile of v1, /device:TPU:1, one launch (start us, length us, event | category | flops | bytes accessed | tf_op | source)
XLA Modules:
  0.0 97.3 jit_solution(6569744317266326281)
XLA Ops:
  0.6 0.0 copy-start
  0.6 5.1 %copy-done = f32[40,64,1281]{2,1,0:T(8,128)S(1)} copy-done((f32[40,64,1281]{2,1,0:T(8,128)S(1)}, f32[40,64,1281]{2,1,0:T(8,128)}, u32[]{:S(2)}) %copy-start) | copy-done | bytes 13117464
  5.7 0.0 copy-start.2
  5.7 1.5 %copy-done.2 = f32[40,2,2,2,1281]{4,3,2,1,0:T(2,128)S(1)} copy-done((f32[40,2,2,2,1281]{4,3,2,1,0:T(2,128)S(1)}, f32[40,2,2,2,1281]{4,3,2,1,0:T(2,128)}, u32[]{:S(2)}) %copy-start.2) | copy-done | bytes 1639704
  7.2 0.0 copy-start.3
  7.2 0.7 copy-done.3
  7.9 0.0 copy-start.5
  7.9 0.7 copy-done.5
  8.6 0.0 copy-start.4
  8.6 0.0 copy-start.6
  8.6 0.0 copy-start.7
  8.6 0.0 copy-start.8
  8.6 9.7 %inverse.1 = f32[128,8,128]{2,1,0:T(8,128)} custom-call(s32[640]{0:T(1024)S(1)} %copy-done.3, s32[128]{0:T(128)S(1)} %copy-done.5, f32[40,2,2,2,1281]{4,3,2,1,0:T(2,128)S(1)} %copy-done.2, f32[40,64,1281]{2,1,0:T(8,128)S(1)} %copy-done), custom_call_target="tpu_custom_call" | custom-call | tf_op jit(solution)/shard_map/inverse/pallas_call | solution.py:303
  18.3 11.5 %all-to-all-start = ((f32[128,8,128]{2,1,0:T(8,128)}), f32[128,8,128]{2,1,0:T(8,128)S(1)}, u32[]{:S(2)}, u32[]{:S(2)}) async-start(f32[128,8,128]{2,1,0:T(8,128)} %inverse.1), calls=%async_computation | async-start | bytes 1048576 | tf_op jit(solution)/shard_map/all_to_all | solution.py:323
  29.8 0.0 copy-done.4
  29.8 0.1 convert_element_type.7.col_ref
  30.0 13.3 %all-to-all-done = f32[128,8,128]{2,1,0:T(8,128)S(1)} async-done(((f32[128,8,128]{2,1,0:T(8,128)}), f32[128,8,128]{2,1,0:T(8,128)S(1)}, u32[]{:S(2)}, u32[]{:S(2)}) %all-to-all-start) | async-done | bytes 524320 | tf_op jit(solution)/shard_map/all_to_all | solution.py:323
  43.3 0.0 copy-done.6
  43.3 0.0 copy-done.7
  43.3 0.0 copy-done.8
  43.3 16.2 %rows.1 = (f32[1,2,16,5248]{3,2,1,0:T(8,128)}, f32[16,128,128]{2,1,0:T(8,128)S(1)}) custom-call(s32[128]{0:T(128)S(1)} %copy-done.6, s32[64]{0:T(128)S(1)} %copy-done.7, f32[64]{0:T(128)S(1)} %copy-done.8, s32[1,640]{1,0:T(1,128)S(1)} %broadcast_in_dim.4.row_ref, f32[640,1]{1,0:T(8,128)S(1)} %convert_element_type.7.col_ref, f32[16,64,128]{2,1,0:T(8,128)S(1)} %bitcast.2), custom_call_target="tpu_custom_call" | custom-call | tf_op jit(solution)/shard_map/rows/pallas_call | solution.py:326
  59.5 23.3 %all_to_all.10.in_ref = f32[128,16,128]{2,1,0:T(8,128)S(1)} all-to-all(f32[128,16,128]{2,1,0:T(8,128)S(1)} %bitcast.3), channel_id=1, replica_groups=mesh['wave'=16,'level'=8] {'wave','level'}, dimensions={0} | all-to-all | bytes 2097152 | tf_op jit(solution)/shard_map/all_to_all | solution.py:356
  82.8 5.1 %copy-done.1 = f32[40,64,1281]{2,1,0:T(8,128)S(1)} copy-done((f32[40,64,1281]{2,1,0:T(8,128)S(1)}, f32[40,64,1281]{2,1,0:T(8,128)}, u32[]{:S(2)}) %copy-start.1) | copy-done | bytes 13117464
  87.9 9.4 %direct.1 = f32[40,5,2,2,1281]{4,3,2,1,0:T(2,128)} custom-call(s32[640]{0:T(1024)S(1)} %copy-done.4, s32[128]{0:T(128)S(1)} %copy-done.6, f32[128,16,128]{2,1,0:T(8,128)S(1)} %all_to_all.10.in_ref, f32[40,64,1281]{2,1,0:T(8,128)S(1)} %copy-done.1), custom_call_target="tpu_custom_call" | custom-call | tf_op jit(solution)/shard_map/direct/pallas_call | solution.py:357
  (3 shorter events, 0.0 us)
Async XLA Ops:
  0.6 5.1 %copy-start = (f32[40,64,1281]{2,1,0:T(8,128)S(1)}, f32[40,64,1281]{2,1,0:T(8,128)}, u32[]{:S(2)}) copy-start(f32[40,64,1281]{2,1,0:T(8,128)} %leg_ref.3) | copy-start | bytes 39352324
  5.7 1.5 %copy-start.2 = (f32[40,2,2,2,1281]{4,3,2,1,0:T(2,128)S(1)}, f32[40,2,2,2,1281]{4,3,2,1,0:T(2,128)}, u32[]{:S(2)}) copy-start(f32[40,2,2,2,1281]{4,3,2,1,0:T(2,128)} %spec_ref.1) | copy-start | bytes 4919044
  7.2 0.7 copy-start.3
  7.9 0.7 copy-start.5
  8.6 21.2 %copy-start.4 = (s32[640]{0:T(1024)S(1)}, s32[640]{0:T(1024)}, u32[]{:S(2)}) copy-start(s32[640]{0:T(1024)} %wave_ref.3) | copy-start | bytes 7684
  8.6 34.7 %copy-start.6 = (s32[128]{0:T(128)S(1)}, s32[128]{0:T(128)}, u32[]{:S(2)}) copy-start(s32[128]{0:T(128)} %band_ref.5) | copy-start | bytes 1540
  8.6 34.7 %copy-start.7 = (s32[64]{0:T(128)S(1)}, s32[64]{0:T(128)}, u32[]{:S(2)}) copy-start(s32[64]{0:T(128)} %len_ref.1) | copy-start | bytes 772
  8.6 34.7 %copy-start.8 = (f32[64]{0:T(128)S(1)}, f32[64]{0:T(128)}, u32[]{:S(2)}) copy-start(f32[64]{0:T(128)} %gauss_ref.1) | copy-start | bytes 772
  18.3 25.0 %all-to-all-start = ((f32[128,8,128]{2,1,0:T(8,128)}), f32[128,8,128]{2,1,0:T(8,128)S(1)}, u32[]{:S(2)}, u32[]{:S(2)}) async-start(f32[128,8,128]{2,1,0:T(8,128)} %inverse.1), calls=%async_computation | async-start | bytes 1048576 | tf_op jit(solution)/shard_map/all_to_all | solution.py:323
  82.8 5.1 %copy-start.1 = (f32[40,64,1281]{2,1,0:T(8,128)S(1)}, f32[40,64,1281]{2,1,0:T(8,128)}, u32[]{:S(2)}) copy-start(f32[40,64,1281]{2,1,0:T(8,128)} %leg_ref.3) | copy-start | bytes 39352324

commit v2 on v1

--- a/solution.py
+++ b/solution.py
@@ -14,6 +14,7 @@
 MIB = 1 << 20
 SIN_TERMS = [(-1.0) ** i / math.factorial(2 * i + 1) for i in range(6)]
 COS_TERMS = [(-1.0) ** i / math.factorial(2 * i) for i in range(7)]
+MESH = pl.DeviceIdType.MESH
 NT = (((1,), (1,)), ((), ()))
 NN = (((1,), (0,)), ((), ()))
 
@@ -43,7 +44,19 @@
     return 1.0 - 2.0 * sine * sine, 2.0 * sine * cosine
 
 
-def inverse_kernel(group, wave_ref, band_ref, spec_ref, leg_ref, out_ref, flat, sums, rows):
+def peer(k):
+    wave, level = lax.axis_index("wave"), lax.axis_index("level")
+    core, y, x, z = k % 2, k // 2 % 4, k // 8 % 4, k // 32
+    return (wave // 4 + z) % 4 * 4 + (wave % 4 + x) % 4, (level // 2 + y) % 4 * 2 + (level % 2 + core) % 2
+
+
+def send(source, target, sems, device):
+    return pltpu.make_async_remote_copy(
+        src_ref=source, dst_ref=target, send_sem=sems.at[0], recv_sem=sems.at[1], device_id=device, device_id_type=MESH
+    )
+
+
+def inverse_step(group, wave_ref, spec_ref, leg_ref, flat, sums):
     step = pl.program_id(0)
     slots = sums.shape[0] // 32
     pack = leg_ref.shape[2]
@@ -71,31 +84,69 @@
         both = both[:32] + both[32:]
         sums[pl.ds(pl.multiple_of(slot * 32, 32), 32), :] = both + pltpu.roll(both, 64, 1)
 
-    @pl.when(step == pl.num_programs(0) - 1)
+
+def sort_rows(band_ref, sums, flat_rows, rows, out_ref):
+    slots = sums.shape[0] // 32
+    north = lax.broadcasted_iota(jnp.int32, (slots, LANES), 1) < 64
+    for c in range(8):
+        v = [sums[pl.ds(8 * i + c, slots, stride=32), :] for i in range(4)]
+        block = jnp.concatenate(
+            [
+                jnp.where(north, v[0], v[1]),
+                jnp.where(north, v[2], v[3]),
+                jnp.zeros((LANES - 2 * slots, LANES), F32),
+            ],
+            axis=0,
+        )
+        flat_rows[pl.ds(c, LANES, stride=8), :] = block.T
+
+    @pl.loop(0, LANES, unroll=8)
+    def _(i):
+        rows[i] = flat_rows[pl.ds(pl.multiple_of(i * 8, 8), 8), :]
+
+    @pl.loop(0, out_ref.shape[0], unroll=8)
+    def _(i):
+        out_ref[i] = rows[band_ref[i]]
+
+
+def main_kernel(
+    group, wave_ref, band_ref, len_ref, gauss_ref, map_ref, spec_ref, leg_ref, segs_ref, out_ref,
+    flat, sums, flat_rows, rows, row_ref, col_ref, send_ref, in_ref, sorted_x, even_x, odd_x, even_l, odd_l,
+    even_hi, even_lo, odd_hi, odd_lo, segs, even_f, odd_f, back, packed, back_ref, sems, back_sems, local_sems,
+):
+    step = pl.program_id(0)
+    steps = pl.num_programs(0)
+    devices = send_ref.shape[0]
+    barrier = pltpu.get_barrier_semaphore()
+
+    for n in range(13):
+        k = step * 13 + n + 1
+
+        @pl.when(k < devices)
+        def _():
+            pl.semaphore_signal(barrier, inc=1, device_id=peer(k), device_id_type=MESH)
+
+    inverse_step(group, wave_ref, spec_ref, leg_ref, flat, sums)
+
+    @pl.when(step == steps - 1)
     def _():
-        north = lax.broadcasted_iota(jnp.int32, (slots, LANES), 1) < 64
-        for c in range(8):
-            v = [sums[pl.ds(8 * i + c, slots, stride=32), :] for i in range(4)]
-            block = jnp.concatenate(
-                [
-                    jnp.where(north, v[0], v[1]),
-                    jnp.where(north, v[2], v[3]),
-                    jnp.zeros((LANES - 2 * slots, LANES), F32),
-                ],
-                axis=0,
-            )
-            rows[pl.ds(c, LANES, stride=8), :] = block.T
-
-        @pl.loop(0, out_ref.shape[0], unroll=8)
-        def _(i):
-            out_ref[i] = rows[pl.ds(pl.multiple_of(band_ref[i] * 8, 8), 8), :]
-
-
-def row_kernel(
-    band_ref, len_ref, gauss_ref, row_ref, col_ref, in_ref, grid_ref, out_ref,
-    sorted_x, even_x, odd_x, even_l, odd_l, even_hi, even_lo, odd_hi, odd_lo, segs, even_f, odd_f, acc, back, packed,
+        sort_rows(band_ref, sums, flat_rows, rows, send_ref)
+        pl.semaphore_wait(barrier, devices - 1)
+        row_part(
+            band_ref, len_ref, gauss_ref, map_ref, row_ref, col_ref, segs_ref, out_ref, send_ref, in_ref, sorted_x,
+            even_x, odd_x, even_l, odd_l, even_hi, even_lo, odd_hi, odd_lo, segs, even_f, odd_f, back, packed,
+            back_ref, sems, back_sems, local_sems,
+        )
+
+
+def row_part(
+    band_ref, len_ref, gauss_ref, map_ref, row_ref, col_ref, segs_ref, out_ref, send_ref, in_ref, sorted_x,
+    even_x, odd_x, even_l, odd_l, even_hi, even_lo, odd_hi, odd_lo, segs, even_f, odd_f, back, packed,
+    back_ref, sems, back_sems, local_sems,
 ):
-    here = lax.axis_index("wave") * lax.axis_size("level") + lax.axis_index("level")
+    my_wave, my_level = lax.axis_index("wave"), lax.axis_index("level")
+    levels = lax.axis_size("level")
+    here = my_wave * levels + my_level
     row = band_ref[here] & 63
     length = len_ref[row]
     quarter = lax.shift_right_logical(length, 2)
@@ -105,16 +156,27 @@
     half_waves = row_ref.shape[1]
     blocks = half_waves // LANES
     devices = in_ref.shape[0]
+    everyone = devices * levels
     share = half_waves // devices
     tiles = even_hi.shape[1] // LANES
     lane = lax.broadcasted_iota(jnp.int32, (1, LANES), 1)
 
-    @pl.loop(0, half_waves // 32)
-    def _(group):
+    mapped = map_ref[...]
+    row_ref[...] = jnp.where((mapped & 1) == 0, mapped, wave_top - mapped)
+    for block in range(blocks):
+        at = slice(block * LANES, (block + 1) * LANES)
+        col_ref[at, :] = jnp.broadcast_to(row_ref[:, at].astype(F32), (LANES, LANES)).T
+
+    def start_send(k):
+        to_wave, to_level = peer(k)
+        mine = in_ref.at[my_wave, pl.ds(pl.multiple_of(my_level * 8, 8), 8), :]
+        send(send_ref.at[to_wave * levels + to_level], mine, sems, (to_wave, to_level)).start()
+
+    def make_tables(group):
         block, inner = group // 4, group % 4
         at_cos = pl.multiple_of(block * 256 + inner * 32, 32)
         at_sin = pl.multiple_of(block * 256 + LANES + inner * 32, 32)
-        evens = jnp.broadcast_to(col_ref[pl.ds(pl.multiple_of(group * 32, 32), 32), :], (32, LANES))
+        evens = col_ref[pl.ds(pl.multiple_of(group * 32, 32), 32), :]
         for waves, table_hi, table_lo in ((evens, even_hi, even_lo), (wave_top - evens, odd_hi, odd_lo)):
             cosine, sine = turn_trig(waves * lane.astype(F32), length_f, inverse)
             turn_cos, turn_sin = turn_trig(waves * float(LANES), length_f, inverse)
@@ -131,6 +193,23 @@
                         cosine * turn_cos - sine * turn_sin,
                         sine * turn_cos + cosine * turn_sin,
                     )
+
+    in_ref[my_wave, pl.ds(pl.multiple_of(my_level * 8, 8), 8), :] = send_ref[here]
+    start_send(1)
+
+    @pl.loop(0, 18)
+    def _(group):
+        for n in range(7):
+            start_send(group * 7 + n + 2)
+        make_tables(group)
+
+    @pl.loop(18, half_waves // 32)
+    def _(group):
+        make_tables(group)
+
+    landed = send_ref.at[pl.ds(0, everyone - 1)]
+    arrival = send(landed, landed, sems, (my_wave, my_level))
+    arrival.wait_recv()
 
     for dev in range(devices):
         for c in range(8):
@@ -190,23 +269,8 @@
                 f_ref[80 * n : 80 * n + 80, at] = high
                 f_ref[160 + 80 * n : 240 + 80 * n, at] = low
 
-    acc[...] = jnp.zeros_like(acc)
-    for i in range(4):
-        begin = i * quarter
-        shift = begin & (LANES - 1)
-        base = lax.shift_right_logical(begin, 7)
-        before = jnp.zeros((32, LANES), F32)
-        for tile in range(tiles + 1):
-            if tile < tiles:
-                rolled = pltpu.roll(segs[i, :, tile * LANES : (tile + 1) * LANES], shift, 1)
-            else:
-                rolled = jnp.zeros((32, LANES), F32)
-            at = pl.ds(pl.multiple_of((base + tile) * LANES, LANES), LANES)
-            acc[:, at] += jnp.where(lane < shift, before, rolled)
-            before = rolled
-    pad_len = grid_ref.shape[3]
-    for f in range(2):
-        grid_ref[0, f] = acc[16 * f : 16 * f + 16, :pad_len]
+    grid_copy = pltpu.make_async_copy(segs, segs_ref, local_sems.at[0])
+    grid_copy.start()
 
     scale = gauss_ref[row] * inverse
     for block in range(blocks):
@@ -237,12 +301,54 @@
             packed[part, 0:16, 2 * share : 3 * share] = even[64:]
             packed[part, 16:32, 2 * share : 3 * share] = odd[64:]
             for n in range(8):
-                out_ref[dev, pl.ds(2 * n + part, 8, stride=16), :] = packed[
+                back_ref[dev, pl.ds(2 * n + part, 8, stride=16), :] = packed[
                     part, pl.ds(n // 2 * 16 + n % 2, 8, stride=2), :
                 ]
 
-
-def direct_kernel(group, wave_ref, band_ref, in_ref, leg_ref, out_ref, natural, turned):
+    own_rows = pl.ds(pl.multiple_of(my_level * 16, 16), 16)
+    own = pltpu.make_async_copy(back_ref.at[my_wave, own_rows, :], out_ref.at[here], local_sems.at[1])
+    own.start()
+
+    @pl.loop(1, everyone)
+    def _(k):
+        to_wave, to_level = peer(k)
+        block = back_ref.at[to_wave, pl.ds(pl.multiple_of(to_level * 16, 16), 16), :]
+        send(block, out_ref.at[here], back_sems, (to_wave, to_level)).start()
+
+    arrival.wait_send()
+    landed = out_ref.at[pl.ds(0, everyone - 1)]
+    arrival = send(landed, landed, back_sems, (my_wave, my_level))
+    arrival.wait_recv()
+    arrival.wait_send()
+    own.wait()
+    grid_copy.wait()
+
+
+def lay_quarters(quarter, segs, acc, grid_ref):
+    tiles = segs.shape[2] // LANES
+    lane = lax.broadcasted_iota(jnp.int32, (1, LANES), 1)
+    acc[...] = jnp.zeros_like(acc)
+    for i in range(4):
+        begin = i * quarter
+        shift = begin & (LANES - 1)
+        base = lax.shift_right_logical(begin, 7)
+        before = jnp.zeros((32, LANES), F32)
+        for tile in range(tiles + 1):
+            if tile < tiles:
+                rolled = pltpu.roll(segs[i, :, tile * LANES : (tile + 1) * LANES], shift, 1)
+            else:
+                rolled = jnp.zeros((32, LANES), F32)
+            at = pl.ds(pl.multiple_of((base + tile) * LANES, LANES), LANES)
+            acc[:, at] += jnp.where(lane < shift, before, rolled)
+            before = rolled
+    pad_len = grid_ref.shape[3]
+    for f in range(2):
+        grid_ref[0, f] = acc[16 * f : 16 * f + 16, :pad_len]
+
+
+def direct_kernel(
+    group, wave_ref, band_ref, len_ref, in_ref, segs_ref, leg_ref, out_ref, grid_ref, natural, turned, acc
+):
     step = pl.program_id(0)
     pack = leg_ref.shape[2]
     slots = pl.num_programs(0) * group
@@ -250,6 +356,9 @@
 
     @pl.when(step == 0)
     def _():
+        row = band_ref[wave_pos * lax.axis_size("level") + lax.axis_index("level")] & 63
+        lay_quarters(lax.shift_right_logical(len_ref[row], 2), segs_ref, acc, grid_ref)
+
         @pl.loop(0, in_ref.shape[0], unroll=8)
         def _(i):
             natural[pl.ds(pl.multiple_of(band_ref[i] * 16, 16), 16), :] = in_ref[i]
@@ -288,7 +397,6 @@
 
 
 def shards(spec_in, legendre, gauss, wave_map, band_map, row_len):
-    axes = ("wave", "level")
     wave_devices = lax.axis_size("wave")
     devices = wave_devices * lax.axis_size("level")
     slots, _, _, _, pack = spec_in.shape
@@ -297,81 +405,92 @@
     pad_len = (20 + 4 * (waves - 1) + 127) // 128 * 128
     table_len = (pad_len // 4 + 127) // 128 * 128
     smem = pl.BlockSpec(memory_space=pltpu.SMEM)
-    vmem = pl.BlockSpec(memory_space=pltpu.VMEM)
     group = 4
 
-    outgoing = pl.pallas_call(
-        functools.partial(inverse_kernel, group),
-        out_shape=jax.ShapeDtypeStruct((devices, 8, LANES), F32),
+    def whole(*shape):
+        return pl.BlockSpec(shape, lambda s: (0,) * len(shape))
+
+    anywhere = pl.BlockSpec(memory_space=pl.ANY)
+    half = waves // 2
+    table = pltpu.VMEM((waves, table_len), BF16)
+    segs, returned = pl.pallas_call(
+        functools.partial(main_kernel, group),
+        out_shape=(
+            jax.ShapeDtypeStruct((4, 32, table_len), F32),
+            jax.ShapeDtypeStruct((devices, 16, LANES), F32),
+        ),
         grid=(slots // group,),
         in_specs=[
             smem,
             smem,
+            smem,
+            smem,
+            whole(1, half),
             pl.BlockSpec((group, 2, 2, 2, pack), lambda s: (s, 0, 0, 0, 0)),
             pl.BlockSpec((group, lat_pairs, pack), lambda s: (s, 0, 0)),
         ],
-        out_specs=pl.BlockSpec((devices, 8, LANES), lambda s: (0, 0, 0)),
+        out_specs=(anywhere, anywhere),
         scratch_shapes=[
             pltpu.VMEM((8, pack), F32),
             pltpu.VMEM((slots * 32, LANES), F32),
             pltpu.VMEM((LANES * 8, LANES), F32),
-        ],
-        compiler_params=pltpu.CompilerParams(vmem_limit_bytes=32 * MIB),
-        name="inverse",
-    )(wave_map, band_map, spec_in, legendre)
-
-    arrived = lax.all_to_all(outgoing, axes, split_axis=0, concat_axis=0, tiled=True)
-    arrived = arrived.reshape(wave_devices, 64, LANES)
-    evens = jnp.where(wave_map % 2 == 0, wave_map, waves - 1 - wave_map)
-    grid_out, returning = pl.pallas_call(
-        row_kernel,
-        out_shape=(
-            jax.ShapeDtypeStruct((1, 2, 16, pad_len), F32),
-            jax.ShapeDtypeStruct((wave_devices, 128, LANES), F32),
-        ),
-        in_specs=[smem, smem, smem, vmem, vmem, vmem],
-        out_specs=(vmem, vmem),
-        scratch_shapes=[
+            pltpu.VMEM((LANES, 8, LANES), F32),
+            pltpu.VMEM((1, half), jnp.int32),
+            pltpu.VMEM((half, LANES), F32),
+            pltpu.VMEM((devices, 8, LANES), F32),
+            pltpu.VMEM((wave_devices, 64, LANES), F32),
             pltpu.VMEM((4, 64, LANES), F32),
-            pltpu.VMEM((64, waves // 2), F32),
-            pltpu.VMEM((64, waves // 2), F32),
+            pltpu.VMEM((64, half), F32),
+            pltpu.VMEM((64, half), F32),
             pltpu.VMEM((256, waves), BF16),
             pltpu.VMEM((256, waves), BF16),
-            pltpu.VMEM((waves, table_len), BF16),
-            pltpu.VMEM((waves, table_len), BF16),
-            pltpu.VMEM((waves, table_len), BF16),
-            pltpu.VMEM((waves, table_len), BF16),
+            table,
+            table,
+            table,
+            table,
             pltpu.VMEM((4, 32, table_len), F32),
             pltpu.VMEM((320, table_len), BF16),
             pltpu.VMEM((320, table_len), BF16),
-            pltpu.VMEM((32, 4 * table_len), F32),
-            pltpu.VMEM((4, 80, waves // 2), F32),
+            pltpu.VMEM((4, 80, half), F32),
             pltpu.VMEM((2, 64, LANES), F32),
+            pltpu.VMEM((wave_devices, 128, LANES), F32),
+            pltpu.SemaphoreType.DMA((2,)),
+            pltpu.SemaphoreType.DMA((2,)),
+            pltpu.SemaphoreType.DMA((2,)),
         ],
-        compiler_params=pltpu.CompilerParams(vmem_limit_bytes=48 * MIB),
+        compiler_params=pltpu.CompilerParams(
+            collective_id=0, has_side_effects=True, vmem_limit_bytes=56 * MIB
+        ),
         name="rows",
-    )(band_map, row_len, gauss, evens[None, :], evens[:, None].astype(F32), arrived)
-
-    returning = returning.reshape(devices, 16, LANES)
-    returned = lax.all_to_all(returning, axes, split_axis=0, concat_axis=0, tiled=True)
-    spec_out = pl.pallas_call(
+    )(wave_map, band_map, row_len, gauss, wave_map[None, :], spec_in, legendre)
+
+    spec_out, grid_out = pl.pallas_call(
         functools.partial(direct_kernel, group),
-        out_shape=jax.ShapeDtypeStruct((slots, 5, 2, 2, pack), F32),
+        out_shape=(
+            jax.ShapeDtypeStruct((slots, 5, 2, 2, pack), F32),
+            jax.ShapeDtypeStruct((1, 2, 16, pad_len), F32),
+        ),
         grid=(slots // group,),
         in_specs=[
             smem,
             smem,
-            pl.BlockSpec((devices, 16, LANES), lambda s: (0, 0, 0)),
+            smem,
+            whole(devices, 16, LANES),
+            whole(4, 32, table_len),
             pl.BlockSpec((group, lat_pairs, pack), lambda s: (s, 0, 0)),
         ],
-        out_specs=pl.BlockSpec((group, 5, 2, 2, pack), lambda s: (s, 0, 0, 0, 0)),
+        out_specs=(
+            pl.BlockSpec((group, 5, 2, 2, pack), lambda s: (s, 0, 0, 0, 0)),
+            whole(1, 2, 16, pad_len),
+        ),
         scratch_shapes=[
             pltpu.VMEM((LANES * 16, LANES), F32),
             pltpu.VMEM((LANES * 16, LANES), F32),
+            pltpu.VMEM((32, 4 * table_len), F32),
         ],
-        compiler_params=pltpu.CompilerParams(vmem_limit_bytes=32 * MIB),
+        compiler_params=pltpu.CompilerParams(vmem_limit_bytes=56 * MIB),
         name="direct",
-    )(wave_map, band_map, returned, legendre)
+    )(wave_map, band_map, row_len, returned, segs, legendre)
     return (grid_out, spec_out)
 
 

time: 97.7 us -> 82.2 us (0.84)
  Pallas kernels: 35.3 us -> 79.7 us
  blocking collectives: 23.3 us -> 0 us
  waiting for transfers between devices: 13.3 us -> 0 us
  local copies, waits for them, and re-layouts: 13.2 us -> 1.27 us
  starting transfers between devices: 11.5 us -> 0 us
    pallas_call x3 -> x2, Pallas kernels: 35.3 us -> 79.7 us  [the longest x1 65.1 us: shards(): pl.pallas_call(functools.partial(main_kernel, group), out_shape=(jax.Shap...]
    all_to_all x1 -> x0, blocking collectives: 23.3 us -> none  [shards(): lax.all_to_all(returning, axes, split_axis=0, concat_axis=0, tiled=True)]
    all_to_all x1 -> x0, waiting for transfers between devices: 13.3 us -> none  [shards(): lax.all_to_all(outgoing, axes, split_axis=0, concat_axis=0, tiled=True)]
    unnamed x18 -> x0, local copies, waits for them, and re-layouts: 13 us -> none
    all_to_all x1 -> x0, starting transfers between devices: 11.5 us -> none  [shards(): lax.all_to_all(outgoing, axes, split_axis=0, concat_axis=0, tiled=True)]
    broadcast_in_dim x1, local copies, waits for them, and re-layouts: 0.01 us -> 1.27 us  [shards(): wave_map[None, :]]
  transfers between devices with their start and end apart: 1 -> 0, of which waited for: 1 -> 0; matrix products, arithmetic and copies ran while one was open for 0% -> 0% of each run, Pallas kernels for 0% -> 0%
where the time goes in v2:
time: 82.2 us; the launch traced here: 81.6 us
  Pallas kernels  79.7 us (97%)
  local copies, waits for them, and re-layouts  1.27 us (2%)
    pallas_call x1, Pallas kernels, shards(): pl.pallas_call(functools.partial(main_kernel, group), out_shape=(jax.Shap...  65.1 us
    pallas_call x1, Pallas kernels, shards(): pl.pallas_call(functools.partial(direct_kernel, group), out_shape=(jax.Sh...  14.6 us

profile of v2, /device:TPU:1, one launch (start us, length us, event | category | flops | bytes accessed | tf_op | source)
XLA Modules:
  0.0 81.6 jit_solution(17008837850145596498)
XLA Ops:
  0.6 1.3 %broadcast_in_dim.3.map_ref = s32[1,640]{1,0:T(1,128)} reshape(s32[640]{0:T(1024)} %wave_ref.3) | data formatting | bytes 5120 | tf_op jit(solution)/shard_map/broadcast_in_dim | solution.py:465
  1.9 65.1 %rows.1 = (f32[4,32,1408]{2,1,0:T(8,128)}, f32[128,16,128]{2,1,0:T(8,128)}) custom-call(s32[640]{0:T(1024)} %wave_ref.3, s32[128]{0:T(128)} %band_ref.3, s32[64]{0:T(128)} %len_ref.3, f32[64]{0:T(128)} %gauss_ref.1, s32[1,640]{1,0:T(1,128)} %broadcast_in_dim.3.map_ref, f32[40,2,2,2,1281]{4,3,2,1,0:T(2,128)} %spec_ref.1, f32[40,64,1281]{2,1,0:T(8,128)} %leg_ref.3), custom_call_target="tpu_custom_call" | custom-call | tf_op jit(solution)/shard_map/rows/pallas_call | solution.py:416
  67.0 14.6 %direct.1 = (f32[40,5,2,2,1281]{4,3,2,1,0:T(2,128)}, f32[1,2,16,5248]{3,2,1,0:T(8,128)}) custom-call(s32[640]{0:T(1024)} %wave_ref.3, s32[128]{0:T(128)} %band_ref.3, s32[64]{0:T(128)} %len_ref.3, f32[128,16,128]{2,1,0:T(8,128)} %get-tuple-element.6.in_ref, f32[4,32,1408]{2,1,0:T(8,128)} %get-tuple-element.7.segs_ref, f32[40,64,1281]{2,1,0:T(8,128)} %leg_ref.3), custom_call_target="tpu_custom_call" | custom-call | tf_op jit(solution)/shard_map/direct/pallas_call | solution.py:467

commit v3 on v2

--- a/solution.py
+++ b/solution.py
@@ -12,11 +12,16 @@
 BF16 = jnp.bfloat16
 LANES = 128
 MIB = 1 << 20
+STEPS = 10
 SIN_TERMS = [(-1.0) ** i / math.factorial(2 * i + 1) for i in range(6)]
 COS_TERMS = [(-1.0) ** i / math.factorial(2 * i) for i in range(7)]
 MESH = pl.DeviceIdType.MESH
 NT = (((1,), (1,)), ((), ()))
 NN = (((1,), (0,)), ((), ()))
+COEF_UNITS = [(f, part, odd) for f in range(2) for part in range(2) for odd in range(2)]
+COEF_ROWS = [COEF_UNITS[i : i + 3] for i in range(0, 8, 3)]
+FLUX_UNITS = [(x, odd) for x in range(5) for odd in range(2)]
+FLUX_ROWS = [FLUX_UNITS[i : i + 3] for i in range(0, 9, 3)]
 
 
 def dot(a, b, dims):
@@ -88,17 +93,19 @@
 def sort_rows(band_ref, sums, flat_rows, rows, out_ref):
     slots = sums.shape[0] // 32
     north = lax.broadcasted_iota(jnp.int32, (slots, LANES), 1) < 64
-    for c in range(8):
-        v = [sums[pl.ds(8 * i + c, slots, stride=32), :] for i in range(4)]
-        block = jnp.concatenate(
-            [
-                jnp.where(north, v[0], v[1]),
-                jnp.where(north, v[2], v[3]),
-                jnp.zeros((LANES - 2 * slots, LANES), F32),
-            ],
-            axis=0,
+
+    def piece(f, lv, part, odd):
+        at = 16 * odd + 4 * f + 2 * lv + part
+        south_at = at + 8
+        return jnp.where(
+            north, sums[pl.ds(at, slots, stride=32), :], sums[pl.ds(south_at, slots, stride=32), :]
         )
-        flat_rows[pl.ds(c, LANES, stride=8), :] = block.T
+
+    for lv in range(2):
+        for j, units in enumerate(COEF_ROWS):
+            pieces = [piece(f, lv, part, odd) for f, part, odd in units]
+            pieces.append(jnp.zeros((LANES - len(units) * slots, LANES), F32))
+            flat_rows[pl.ds(3 * lv + j, LANES, stride=8), :] = jnp.concatenate(pieces, axis=0).T
 
     @pl.loop(0, LANES, unroll=8)
     def _(i):
@@ -112,36 +119,35 @@
 def main_kernel(
     group, wave_ref, band_ref, len_ref, gauss_ref, map_ref, spec_ref, leg_ref, segs_ref, out_ref,
     flat, sums, flat_rows, rows, row_ref, col_ref, send_ref, in_ref, sorted_x, even_x, odd_x, even_l, odd_l,
-    even_hi, even_lo, odd_hi, odd_lo, segs, even_f, odd_f, back, packed, back_ref, sems, back_sems, local_sems,
+    even_hi, even_lo, odd_hi, odd_lo, segs, turned, even_f, odd_f, back, packed, back_ref, sems, back_sems, local_sems,
 ):
     step = pl.program_id(0)
-    steps = pl.num_programs(0)
     devices = send_ref.shape[0]
     barrier = pltpu.get_barrier_semaphore()
 
-    for n in range(13):
-        k = step * 13 + n + 1
-
-        @pl.when(k < devices)
-        def _():
+    greeted = (devices - 1) // STEPS
+    for n in range(greeted):
+        k = step * greeted + n + 1
+        pl.semaphore_signal(barrier, inc=1, device_id=peer(k), device_id_type=MESH)
+
+    inverse_step(group, wave_ref, spec_ref, leg_ref, flat, sums)
+
+    @pl.when(step == STEPS - 1)
+    def _():
+        for k in range(STEPS * greeted + 1, devices):
             pl.semaphore_signal(barrier, inc=1, device_id=peer(k), device_id_type=MESH)
-
-    inverse_step(group, wave_ref, spec_ref, leg_ref, flat, sums)
-
-    @pl.when(step == steps - 1)
-    def _():
         sort_rows(band_ref, sums, flat_rows, rows, send_ref)
         pl.semaphore_wait(barrier, devices - 1)
         row_part(
             band_ref, len_ref, gauss_ref, map_ref, row_ref, col_ref, segs_ref, out_ref, send_ref, in_ref, sorted_x,
-            even_x, odd_x, even_l, odd_l, even_hi, even_lo, odd_hi, odd_lo, segs, even_f, odd_f, back, packed,
+            even_x, odd_x, even_l, odd_l, even_hi, even_lo, odd_hi, odd_lo, segs, turned, even_f, odd_f, back, packed,
             back_ref, sems, back_sems, local_sems,
         )
 
 
 def row_part(
     band_ref, len_ref, gauss_ref, map_ref, row_ref, col_ref, segs_ref, out_ref, send_ref, in_ref, sorted_x,
-    even_x, odd_x, even_l, odd_l, even_hi, even_lo, odd_hi, odd_lo, segs, even_f, odd_f, back, packed,
+    even_x, odd_x, even_l, odd_l, even_hi, even_lo, odd_hi, odd_lo, segs, turned, even_f, odd_f, back, packed,
     back_ref, sems, back_sems, local_sems,
 ):
     my_wave, my_level = lax.axis_index("wave"), lax.axis_index("level")
@@ -169,8 +175,8 @@
 
     def start_send(k):
         to_wave, to_level = peer(k)
-        mine = in_ref.at[my_wave, pl.ds(pl.multiple_of(my_level * 8, 8), 8), :]
-        send(send_ref.at[to_wave * levels + to_level], mine, sems, (to_wave, to_level)).start()
+        mine = in_ref.at[my_wave, pl.ds(pl.multiple_of(my_level * 8, 8), 6), :]
+        send(send_ref.at[to_wave * levels + to_level, pl.ds(0, 6), :], mine, sems, (to_wave, to_level)).start()
 
     def make_tables(group):
         block, inner = group // 4, group % 4
@@ -197,28 +203,29 @@
     in_ref[my_wave, pl.ds(pl.multiple_of(my_level * 8, 8), 8), :] = send_ref[here]
     start_send(1)
 
-    @pl.loop(0, 18)
+    @pl.loop(0, 9)
     def _(group):
-        for n in range(7):
-            start_send(group * 7 + n + 2)
+        for n in range(14):
+            start_send(group * 14 + n + 2)
         make_tables(group)
 
-    @pl.loop(18, half_waves // 32)
+    @pl.loop(9, half_waves // 32)
     def _(group):
         make_tables(group)
 
-    landed = send_ref.at[pl.ds(0, everyone - 1)]
+    landed = send_ref.at[pl.ds(0, everyone - 1), pl.ds(0, 6), :]
     arrival = send(landed, landed, sems, (my_wave, my_level))
     arrival.wait_recv()
 
     for dev in range(devices):
-        for c in range(8):
-            f, lv, part = c // 4, c // 2 % 2, c % 2
-            piece = in_ref[dev, pl.ds(c, 8, stride=8), :]
-            sorted_x[dev % 4, pl.ds(32 * part + 16 * f + lv, 8, stride=2), :] = piece
         at = slice(dev * share, (dev + 1) * share)
-        even_x[:, at] = sorted_x[dev % 4, :, :share]
-        odd_x[:, at] = sorted_x[dev % 4, :, share : 2 * share]
+        for j, units in enumerate(COEF_ROWS):
+            for lv in range(2):
+                sorted_x[dev % 4, j, pl.ds(lv, 8, stride=2), :] = in_ref[dev, pl.ds(3 * lv + j, 8, stride=8), :]
+            for n, (f, part, odd) in enumerate(units):
+                to = slice(32 * part + 16 * f, 32 * part + 16 * f + 16)
+                x_ref = odd_x if odd else even_x
+                x_ref[to, at] = sorted_x[dev % 4, j, :, n * share : (n + 1) * share]
 
     highest = jnp.minimum(wave_top, lax.shift_right_logical(length - 1, 1))
     for block in range(blocks):
@@ -269,20 +276,18 @@
                 f_ref[80 * n : 80 * n + 80, at] = high
                 f_ref[160 + 80 * n : 240 + 80 * n, at] = low
 
-    grid_copy = pltpu.make_async_copy(segs, segs_ref, local_sems.at[0])
-    grid_copy.start()
-
     scale = gauss_ref[row] * inverse
-    for block in range(blocks):
-        at = slice(block * LANES, (block + 1) * LANES)
-        rows = slice(block * 256, (block + 1) * 256)
+
+    def fourier_sums(block):
+        at = pl.ds(pl.multiple_of(block * LANES, LANES), LANES)
+        rows = pl.ds(pl.multiple_of(block * 256, 256), 256)
         evens = row_ref[:, at]
         for odd, f_ref, table_hi, table_lo in ((0, even_f, even_hi, even_lo), (1, odd_f, odd_hi, odd_lo)):
             whole = dot(f_ref[...], table_hi[rows, :], NT)
             total = whole[:160] + whole[160:] + dot(f_ref[0:160, :], table_lo[rows, :], NT)
-            wave = wave_top - evens if odd else evens
-            kept = jnp.where(wave <= highest, scale, 0.0)
-            flip = (1 - (wave & 2)).astype(F32)
+            waves = wave_top - evens if odd else evens
+            kept = jnp.where(waves <= highest, scale, 0.0)
+            flip = (1 - (waves & 2)).astype(F32)
             first_cos, first_sin = total[:80, :LANES], total[:80, LANES:]
             second_cos, second_sin = total[80:, :LANES] * flip, total[80:, LANES:] * flip
             if odd:
@@ -292,31 +297,81 @@
                 back[0, :, at] = (first_cos + second_cos) * kept
                 back[1, :, at] = -(first_sin + second_sin) * kept
 
-    for dev in range(devices):
-        at = slice(dev * share, (dev + 1) * share)
+    def send_back(dev):
+        begin = dev * share
+        base = lax.shift_right_logical(begin, 7)
+        offset = begin & (LANES - 1)
+        tiles_at = [pl.ds(pl.multiple_of((base + n) * LANES, LANES), LANES) for n in range(2)]
+
+        def unit(x, odd, part, place):
+            to = place * share
+            shift = (to - offset + LANES) & (LANES - 1)
+            rolled = [pltpu.roll(back[2 * odd + part, 16 * x : 16 * x + 16, at], shift, 1) for at in tiles_at]
+            return jnp.where(lane - to + offset < LANES, rolled[0], rolled[1])
+
+        def joined(units):
+            value = units[0]
+            for n, other in enumerate(units[1:]):
+                value = jnp.where(lane < (n + 1) * share, value, other)
+            return value
+
         for part in range(2):
-            even, odd = back[part, :, at], back[2 + part, :, at]
-            packed[part, :, 0:share] = even[:64]
-            packed[part, :, share : 2 * share] = odd[:64]
-            packed[part, 0:16, 2 * share : 3 * share] = even[64:]
-            packed[part, 16:32, 2 * share : 3 * share] = odd[64:]
-            for n in range(8):
-                back_ref[dev, pl.ds(2 * n + part, 8, stride=16), :] = packed[
-                    part, pl.ds(n // 2 * 16 + n % 2, 8, stride=2), :
-                ]
+            for j, units in enumerate(FLUX_ROWS):
+                packed[3 * part + j] = joined([unit(x, odd, part, n) for n, (x, odd) in enumerate(units)])
+        packed[6] = joined([unit(4, 1, part, part) for part in range(2)])
+        for lv in range(2):
+            for part in range(2):
+                for j in range(3):
+                    back_ref[dev, pl.ds(6 * lv + 3 * part + j, 8, stride=16), :] = packed[
+                        3 * part + j, pl.ds(lv, 8, stride=2), :
+                    ]
+            back_ref[dev, pl.ds(12 + lv, 8, stride=16), :] = packed[6, pl.ds(lv, 8, stride=2), :]
+
+        def start_block(to_level):
+            block = back_ref.at[dev, pl.ds(pl.multiple_of(to_level * 16, 16), 14), :]
+            send(block, out_ref.at[here, pl.ds(0, 14), :], back_sems, (dev, to_level)).start()
+
+        for n in range(1, 8):
+            start_block((my_level + n) % levels)
+
+        @pl.when(dev != my_wave)
+        def _():
+            start_block(my_level)
+
+    first = my_wave * blocks // devices
+
+    @pl.loop(0, blocks)
+    def _(turn):
+        block = (turn + first) % blocks
+        fourier_sums(block)
+        low = jnp.where((turn == 0) & (block > 0), 3 * block + 1, 3 * block)
+        high = jnp.where(block == blocks - 1, devices, 3 * block + 3)
+
+        @pl.loop(low, high)
+        def _(dev):
+            send_back(dev)
+
+        @pl.when((turn == blocks - 1) & (first > 0))
+        def _():
+            send_back(3 * first)
 
     own_rows = pl.ds(pl.multiple_of(my_level * 16, 16), 16)
     own = pltpu.make_async_copy(back_ref.at[my_wave, own_rows, :], out_ref.at[here], local_sems.at[1])
     own.start()
 
-    @pl.loop(1, everyone)
-    def _(k):
-        to_wave, to_level = peer(k)
-        block = back_ref.at[to_wave, pl.ds(pl.multiple_of(to_level * 16, 16), 16), :]
-        send(block, out_ref.at[here], back_sems, (to_wave, to_level)).start()
+    for i in range(4):
+        shift = (i * quarter) & (LANES - 1)
+        before = jnp.zeros((32, LANES), F32)
+        for tile in range(tiles + 1):
+            at = slice(tile * LANES, (tile + 1) * LANES)
+            rolled = pltpu.roll(segs[i, :, at], shift, 1) if tile < tiles else jnp.zeros((32, LANES), F32)
+            turned[i, :, at] = jnp.where(lane < shift, before, rolled)
+            before = rolled
+    grid_copy = pltpu.make_async_copy(turned, segs_ref, local_sems.at[0])
+    grid_copy.start()
 
     arrival.wait_send()
-    landed = out_ref.at[pl.ds(0, everyone - 1)]
+    landed = out_ref.at[pl.ds(0, everyone - 1), pl.ds(0, 14), :]
     arrival = send(landed, landed, back_sems, (my_wave, my_level))
     arrival.wait_recv()
     arrival.wait_send()
@@ -325,23 +380,13 @@
 
 
 def lay_quarters(quarter, segs, acc, grid_ref):
-    tiles = segs.shape[2] // LANES
-    lane = lax.broadcasted_iota(jnp.int32, (1, LANES), 1)
+    pad_len = grid_ref.shape[3]
     acc[...] = jnp.zeros_like(acc)
     for i in range(4):
-        begin = i * quarter
-        shift = begin & (LANES - 1)
-        base = lax.shift_right_logical(begin, 7)
-        before = jnp.zeros((32, LANES), F32)
-        for tile in range(tiles + 1):
-            if tile < tiles:
-                rolled = pltpu.roll(segs[i, :, tile * LANES : (tile + 1) * LANES], shift, 1)
-            else:
-                rolled = jnp.zeros((32, LANES), F32)
+        base = lax.shift_right_logical(i * quarter, 7)
+        for tile in range(segs.shape[2] // LANES):
             at = pl.ds(pl.multiple_of((base + tile) * LANES, LANES), LANES)
-            acc[:, at] += jnp.where(lane < shift, before, rolled)
-            before = rolled
-    pad_len = grid_ref.shape[3]
+            acc[:, at] += segs[i, :, tile * LANES : (tile + 1) * LANES]
     for f in range(2):
         grid_ref[0, f] = acc[16 * f : 16 * f + 16, :pad_len]
 
@@ -351,7 +396,7 @@
 ):
     step = pl.program_id(0)
     pack = leg_ref.shape[2]
-    slots = pl.num_programs(0) * group
+    slots = STEPS * group
     wave_pos = lax.axis_index("wave")
 
     @pl.when(step == 0)
@@ -363,8 +408,14 @@
         def _(i):
             natural[pl.ds(pl.multiple_of(band_ref[i] * 16, 16), 16), :] = in_ref[i]
 
-        for n in range(16):
-            turned[pl.ds(n, LANES, stride=16), :] = natural[pl.ds(n, LANES, stride=16), :].T
+        for lv in range(2):
+            lines = [(3 * p + j, p, FLUX_ROWS[j]) for p in range(2) for j in range(3)]
+            for line, part, units in [(6 * lv + n, p, u) for n, p, u in lines] + [(12 + lv, None, ())]:
+                block = natural[pl.ds(line, LANES, stride=16), :].T
+                placed = [(x, odd, part) for x, odd in units] or [(4, 1, 0), (4, 1, 1)]
+                for n, (x, odd, p) in enumerate(placed):
+                    to = 4 * x + 2 * lv + p + (16 if x < 4 else 4) * odd + (16 if x == 4 else 0)
+                    turned[pl.ds(to, slots, stride=40), :] = block[n * slots : (n + 1) * slots]
 
     position = lax.broadcasted_iota(jnp.int32, (1, pack), 1)
     south = lax.broadcasted_iota(jnp.int32, (1, LANES), 1) >= 64
@@ -373,10 +424,7 @@
         first_wave = wave_ref[wave_pos * slots + slot]
         boundary = (pack - 1) - first_wave
 
-        def of_lane(extra, count):
-            return turned[pl.ds(pl.multiple_of((slot + extra) * 16, 16), count), :]
-
-        x = jnp.concatenate([of_lane(0, 16), of_lane(slots, 16), of_lane(2 * slots, 8)], axis=0)
+        x = turned[pl.ds(pl.multiple_of(slot * 40, 8), 40), :]
         other = pltpu.roll(x, 64, 1)
         difference = x - other
         y = jnp.concatenate([x + other, jnp.where(south, -difference, difference)], axis=0)
@@ -405,7 +453,7 @@
     pad_len = (20 + 4 * (waves - 1) + 127) // 128 * 128
     table_len = (pad_len // 4 + 127) // 128 * 128
     smem = pl.BlockSpec(memory_space=pltpu.SMEM)
-    group = 4
+    group = slots // STEPS
 
     def whole(*shape):
         return pl.BlockSpec(shape, lambda s: (0,) * len(shape))
@@ -416,7 +464,7 @@
     segs, returned = pl.pallas_call(
         functools.partial(main_kernel, group),
         out_shape=(
-            jax.ShapeDtypeStruct((4, 32, table_len), F32),
+            jax.ShapeDtypeStruct((4, 32, table_len + LANES), F32),
             jax.ShapeDtypeStruct((devices, 16, LANES), F32),
         ),
         grid=(slots // group,),
@@ -439,7 +487,7 @@
             pltpu.VMEM((half, LANES), F32),
             pltpu.VMEM((devices, 8, LANES), F32),
             pltpu.VMEM((wave_devices, 64, LANES), F32),
-            pltpu.VMEM((4, 64, LANES), F32),
+            pltpu.VMEM((4, 3, 16, LANES), F32),
             pltpu.VMEM((64, half), F32),
             pltpu.VMEM((64, half), F32),
             pltpu.VMEM((256, waves), BF16),
@@ -449,10 +497,11 @@
             table,
             table,
             pltpu.VMEM((4, 32, table_len), F32),
+            pltpu.VMEM((4, 32, table_len + LANES), F32),
             pltpu.VMEM((320, table_len), BF16),
             pltpu.VMEM((320, table_len), BF16),
-            pltpu.VMEM((4, 80, half), F32),
-            pltpu.VMEM((2, 64, LANES), F32),
+            pltpu.VMEM((4, 80, half + LANES), F32),
+            pltpu.VMEM((7, 16, LANES), F32),
             pltpu.VMEM((wave_devices, 128, LANES), F32),
             pltpu.SemaphoreType.DMA((2,)),
             pltpu.SemaphoreType.DMA((2,)),
@@ -476,7 +525,7 @@
             smem,
             smem,
             whole(devices, 16, LANES),
-            whole(4, 32, table_len),
+            whole(4, 32, table_len + LANES),
             pl.BlockSpec((group, lat_pairs, pack), lambda s: (s, 0, 0)),
         ],
         out_specs=(
@@ -485,7 +534,7 @@
         ),
         scratch_shapes=[
             pltpu.VMEM((LANES * 16, LANES), F32),
-            pltpu.VMEM((LANES * 16, LANES), F32),
+            pltpu.VMEM((slots * 40, LANES), F32),
             pltpu.VMEM((32, 4 * table_len), F32),
         ],
         compiler_params=pltpu.CompilerParams(vmem_limit_bytes=56 * MIB),

time: 82.2 us -> 73.6 us (0.90)
  Pallas kernels: 79.7 us -> 71.1 us
    pallas_call x1, Pallas kernels: 65.1 us -> 56.7 us  [shards(): pl.pallas_call(functools.partial(main_kernel, group), out_shape=(jax.Shap...]
where the time goes in v3:
time: 73.6 us; the launch traced here: 73 us
  Pallas kernels  71.1 us (97%)
  local copies, waits for them, and re-layouts  1.27 us (2%)
    pallas_call x1, Pallas kernels, shards(): pl.pallas_call(functools.partial(main_kernel, group), out_shape=(jax.Shap...  56.7 us
    pallas_call x1, Pallas kernels, shards(): pl.pallas_call(functools.partial(direct_kernel, group), out_shape=(jax.Sh...  14.4 us

profile of v3, /device:TPU:1, one launch (start us, length us, event | category | flops | bytes accessed | tf_op | source)
XLA Modules:
  0.0 73.0 jit_solution(13079169788691340510)
XLA Ops:
  0.6 1.3 %broadcast_in_dim.3.map_ref = s32[1,640]{1,0:T(1,128)} reshape(s32[640]{0:T(1024)} %wave_ref.3) | data formatting | bytes 5120 | tf_op jit(solution)/shard_map/broadcast_in_dim | solution.py:514
  1.9 56.7 %rows.1 = (f32[4,32,1536]{2,1,0:T(8,128)}, f32[128,16,128]{2,1,0:T(8,128)}) custom-call(s32[640]{0:T(1024)} %wave_ref.3, s32[128]{0:T(128)} %band_ref.3, s32[64]{0:T(128)} %len_ref.3, f32[64]{0:T(128)} %gauss_ref.1, s32[1,640]{1,0:T(1,128)} %broadcast_in_dim.3.map_ref, f32[40,2,2,2,1281]{4,3,2,1,0:T(2,128)} %spec_ref.1, f32[40,64,1281]{2,1,0:T(8,128)} %leg_ref.3), custom_call_target="tpu_custom_call" | custom-call | tf_op jit(solution)/shard_map/rows/pallas_call | solution.py:464
  58.6 14.4 %direct.1 = (f32[40,5,2,2,1281]{4,3,2,1,0:T(2,128)}, f32[1,2,16,5248]{3,2,1,0:T(8,128)}) custom-call(s32[640]{0:T(1024)} %wave_ref.3, s32[128]{0:T(128)} %band_ref.3, s32[64]{0:T(128)} %len_ref.3, f32[128,16,128]{2,1,0:T(8,128)} %get-tuple-element.6.in_ref, f32[4,32,1536]{2,1,0:T(8,128)} %get-tuple-element.7.segs_ref, f32[40,64,1281]{2,1,0:T(8,128)} %leg_ref.3), custom_call_target="tpu_custom_call" | custom-call | tf_op jit(solution)/shard_map/direct/pallas_call | solution.py:516

commit v4 on v3

--- a/solution.py
+++ b/solution.py
@@ -61,8 +61,18 @@
     )
 
 
-def inverse_step(group, wave_ref, spec_ref, leg_ref, flat, sums):
-    step = pl.program_id(0)
+def group_copies(group, sources, targets, sems):
+    def copies(n):
+        at = pl.ds(n * group, group)
+        return [
+            pltpu.make_async_copy(source.at[at], target.at[at], sems.at[i, n])
+            for i, (source, target) in enumerate(zip(sources, targets))
+        ]
+
+    return copies
+
+
+def inverse_step(step, group, wave_ref, spec_ref, leg_ref, flat, sums):
     slots = sums.shape[0] // 32
     pack = leg_ref.shape[2]
     wave_pos = lax.axis_index("wave")
@@ -72,8 +82,8 @@
         first_wave = wave_ref[wave_pos * slots + slot]
         boundary = (pack - 1) - first_wave
         for pair in range(4):
-            flat[2 * pair : 2 * pair + 2, :] = spec_ref[g, pair // 2, pair % 2]
-        x = flat[...]
+            flat[g, 2 * pair : 2 * pair + 2, :] = spec_ref[slot, pair // 2, pair % 2]
+        x = flat[g]
         in_first = position < boundary
         parity = jnp.where(in_first, position, position + boundary) & 1
         in_even = in_first == ((first_wave & 1) == 0)
@@ -84,7 +94,7 @@
             for kept in (in_even, jnp.logical_not(in_even)):
                 parts += [jnp.where(kept, part, 0.0), jnp.where(kept, signed, 0.0)]
         left = jnp.concatenate(parts, axis=0).astype(BF16)
-        right = jnp.concatenate(split(leg_ref[g]), axis=0)
+        right = jnp.concatenate(split(leg_ref[slot]), axis=0)
         both = dot(left, right, NT)
         both = both[:32] + both[32:]
         sums[pl.ds(pl.multiple_of(slot * 32, 32), 32), :] = both + pltpu.roll(both, 64, 1)
@@ -117,32 +127,39 @@
 
 
 def main_kernel(
-    group, wave_ref, band_ref, len_ref, gauss_ref, map_ref, spec_ref, leg_ref, segs_ref, out_ref,
+    group, wave_ref, band_ref, len_ref, gauss_ref, map_ref, spec_hbm, leg_hbm, segs_ref, out_ref, spec_ref, leg_ref,
     flat, sums, flat_rows, rows, row_ref, col_ref, send_ref, in_ref, sorted_x, even_x, odd_x, even_l, odd_l,
-    even_hi, even_lo, odd_hi, odd_lo, segs, turned, even_f, odd_f, back, packed, back_ref, sems, back_sems, local_sems,
+    even_hi, even_lo, odd_hi, odd_lo, segs, turned, even_f, odd_f, back, packed, back_ref,
+    load_sems, sems, back_sems, local_sems,
 ):
-    step = pl.program_id(0)
     devices = send_ref.shape[0]
     barrier = pltpu.get_barrier_semaphore()
-
+    copies = group_copies(group, (spec_hbm, leg_hbm), (spec_ref, leg_ref), load_sems)
+    for n in range(STEPS):
+        for copy in copies(n):
+            copy.start()
     greeted = (devices - 1) // STEPS
-    for n in range(greeted):
-        k = step * greeted + n + 1
+
+    def greet(k):
         pl.semaphore_signal(barrier, inc=1, device_id=peer(k), device_id_type=MESH)
 
-    inverse_step(group, wave_ref, spec_ref, leg_ref, flat, sums)
-
-    @pl.when(step == STEPS - 1)
-    def _():
-        for k in range(STEPS * greeted + 1, devices):
-            pl.semaphore_signal(barrier, inc=1, device_id=peer(k), device_id_type=MESH)
-        sort_rows(band_ref, sums, flat_rows, rows, send_ref)
-        pl.semaphore_wait(barrier, devices - 1)
-        row_part(
-            band_ref, len_ref, gauss_ref, map_ref, row_ref, col_ref, segs_ref, out_ref, send_ref, in_ref, sorted_x,
-            even_x, odd_x, even_l, odd_l, even_hi, even_lo, odd_hi, odd_lo, segs, turned, even_f, odd_f, back, packed,
-            back_ref, sems, back_sems, local_sems,
-        )
+    @pl.loop(0, STEPS)
+    def _(step):
+        for copy in copies(step):
+            copy.wait()
+        for n in range(greeted):
+            greet(step * greeted + n + 1)
+        inverse_step(step, group, wave_ref, spec_ref, leg_ref, flat, sums)
+
+    for k in range(STEPS * greeted + 1, devices):
+        greet(k)
+    sort_rows(band_ref, sums, flat_rows, rows, send_ref)
+    pl.semaphore_wait(barrier, devices - 1)
+    row_part(
+        band_ref, len_ref, gauss_ref, map_ref, row_ref, col_ref, segs_ref, out_ref, send_ref, in_ref, sorted_x,
+        even_x, odd_x, even_l, odd_l, even_hi, even_lo, odd_hi, odd_lo, segs, turned, even_f, odd_f, back, packed,
+        back_ref, sems, back_sems, local_sems,
+    )
 
 
 def row_part(
@@ -392,56 +409,69 @@
 
 
 def direct_kernel(
-    group, wave_ref, band_ref, len_ref, in_ref, segs_ref, leg_ref, out_ref, grid_ref, natural, turned, acc
+    group, wave_ref, band_ref, len_ref, in_ref, segs_ref, leg_hbm, spec_hbm, grid_hbm,
+    leg_ref, spec_ref, grid_ref, natural, turned, acc, load_sems, store_sems, grid_sem,
 ):
-    step = pl.program_id(0)
     pack = leg_ref.shape[2]
     slots = STEPS * group
     wave_pos = lax.axis_index("wave")
-
-    @pl.when(step == 0)
-    def _():
-        row = band_ref[wave_pos * lax.axis_size("level") + lax.axis_index("level")] & 63
-        lay_quarters(lax.shift_right_logical(len_ref[row], 2), segs_ref, acc, grid_ref)
-
-        @pl.loop(0, in_ref.shape[0], unroll=8)
-        def _(i):
-            natural[pl.ds(pl.multiple_of(band_ref[i] * 16, 16), 16), :] = in_ref[i]
-
-        for lv in range(2):
-            lines = [(3 * p + j, p, FLUX_ROWS[j]) for p in range(2) for j in range(3)]
-            for line, part, units in [(6 * lv + n, p, u) for n, p, u in lines] + [(12 + lv, None, ())]:
-                block = natural[pl.ds(line, LANES, stride=16), :].T
-                placed = [(x, odd, part) for x, odd in units] or [(4, 1, 0), (4, 1, 1)]
-                for n, (x, odd, p) in enumerate(placed):
-                    to = 4 * x + 2 * lv + p + (16 if x < 4 else 4) * odd + (16 if x == 4 else 0)
-                    turned[pl.ds(to, slots, stride=40), :] = block[n * slots : (n + 1) * slots]
+    loads = group_copies(group, (leg_hbm,), (leg_ref,), load_sems)
+    stores = group_copies(group, (spec_ref,), (spec_hbm,), store_sems)
+    for n in range(STEPS):
+        loads(n)[0].start()
+
+    @pl.loop(0, in_ref.shape[0], unroll=8)
+    def _(i):
+        natural[pl.ds(pl.multiple_of(band_ref[i] * 16, 16), 16), :] = in_ref[i]
+
+    for lv in range(2):
+        lines = [(3 * p + j, p, FLUX_ROWS[j]) for p in range(2) for j in range(3)]
+        for line, part, units in [(6 * lv + n, p, u) for n, p, u in lines] + [(12 + lv, None, ())]:
+            block = natural[pl.ds(line, LANES, stride=16), :].T
+            placed = [(x, odd, part) for x, odd in units] or [(4, 1, 0), (4, 1, 1)]
+            for n, (x, odd, p) in enumerate(placed):
+                to = 4 * x + 2 * lv + p + (16 if x < 4 else 4) * odd + (16 if x == 4 else 0)
+                turned[pl.ds(to, slots, stride=40), :] = block[n * slots : (n + 1) * slots]
+
+    row = band_ref[wave_pos * lax.axis_size("level") + lax.axis_index("level")] & 63
+    lay_quarters(lax.shift_right_logical(len_ref[row], 2), segs_ref, acc, grid_ref)
+    grid_copy = pltpu.make_async_copy(grid_ref, grid_hbm, grid_sem)
+    grid_copy.start()
 
     position = lax.broadcasted_iota(jnp.int32, (1, pack), 1)
     south = lax.broadcasted_iota(jnp.int32, (1, LANES), 1) >= 64
-    for g in range(group):
-        slot = step * group + g
-        first_wave = wave_ref[wave_pos * slots + slot]
-        boundary = (pack - 1) - first_wave
-
-        x = turned[pl.ds(pl.multiple_of(slot * 40, 8), 40), :]
-        other = pltpu.roll(x, 64, 1)
-        difference = x - other
-        y = jnp.concatenate([x + other, jnp.where(south, -difference, difference)], axis=0)
-        left = jnp.concatenate(split(y), axis=0)
-        right = jnp.concatenate(split(leg_ref[g]), axis=0)
-        both = dot(left, right, NN)
-        both = both[:80] + both[80:]
-        in_first = position < boundary
-        parity = jnp.where(in_first, position, position + boundary) & 1
-        in_even = in_first == ((first_wave & 1) == 0)
-        chosen = jnp.where(parity == 0, both[:40], both[40:])
-        main = jnp.where(in_even, chosen[:16], chosen[16:32])
-        last = jnp.where(in_even, chosen[32:36], chosen[36:40])
-        for n in range(8):
-            out_ref[g, n // 2, n % 2] = main[2 * n : 2 * n + 2]
-        for n in range(2):
-            out_ref[g, 4, n] = last[2 * n : 2 * n + 2]
+
+    @pl.loop(0, STEPS)
+    def _(step):
+        loads(step)[0].wait()
+        for g in range(group):
+            slot = step * group + g
+            first_wave = wave_ref[wave_pos * slots + slot]
+            boundary = (pack - 1) - first_wave
+
+            x = turned[pl.ds(pl.multiple_of(slot * 40, 8), 40), :]
+            other = pltpu.roll(x, 64, 1)
+            difference = x - other
+            y = jnp.concatenate([x + other, jnp.where(south, -difference, difference)], axis=0)
+            left = jnp.concatenate(split(y), axis=0)
+            right = jnp.concatenate(split(leg_ref[slot]), axis=0)
+            both = dot(left, right, NN)
+            both = both[:80] + both[80:]
+            in_first = position < boundary
+            parity = jnp.where(in_first, position, position + boundary) & 1
+            in_even = in_first == ((first_wave & 1) == 0)
+            chosen = jnp.where(parity == 0, both[:40], both[40:])
+            main = jnp.where(in_even, chosen[:16], chosen[16:32])
+            last = jnp.where(in_even, chosen[32:36], chosen[36:40])
+            for n in range(8):
+                spec_ref[slot, n // 2, n % 2] = main[2 * n : 2 * n + 2]
+            for n in range(2):
+                spec_ref[slot, 4, n] = last[2 * n : 2 * n + 2]
+        stores(step)[0].start()
+
+    for n in range(STEPS):
+        stores(n)[0].wait()
+    grid_copy.wait()
 
 
 def shards(spec_in, legendre, gauss, wave_map, band_map, row_len):
@@ -455,9 +485,7 @@
     smem = pl.BlockSpec(memory_space=pltpu.SMEM)
     group = slots // STEPS
 
-    def whole(*shape):
-        return pl.BlockSpec(shape, lambda s: (0,) * len(shape))
-
+    vmem = pl.BlockSpec(memory_space=pltpu.VMEM)
     anywhere = pl.BlockSpec(memory_space=pl.ANY)
     half = waves // 2
     table = pltpu.VMEM((waves, table_len), BF16)
@@ -467,19 +495,20 @@
             jax.ShapeDtypeStruct((4, 32, table_len + LANES), F32),
             jax.ShapeDtypeStruct((devices, 16, LANES), F32),
         ),
-        grid=(slots // group,),
         in_specs=[
             smem,
             smem,
             smem,
             smem,
-            whole(1, half),
-            pl.BlockSpec((group, 2, 2, 2, pack), lambda s: (s, 0, 0, 0, 0)),
-            pl.BlockSpec((group, lat_pairs, pack), lambda s: (s, 0, 0)),
+            vmem,
+            anywhere,
+            anywhere,
         ],
         out_specs=(anywhere, anywhere),
         scratch_shapes=[
-            pltpu.VMEM((8, pack), F32),
+            pltpu.VMEM((slots, 2, 2, 2, pack), F32),
+            pltpu.VMEM((slots, lat_pairs, pack), F32),
+            pltpu.VMEM((group, 8, pack), F32),
             pltpu.VMEM((slots * 32, LANES), F32),
             pltpu.VMEM((LANES * 8, LANES), F32),
             pltpu.VMEM((LANES, 8, LANES), F32),
@@ -503,6 +532,7 @@
             pltpu.VMEM((4, 80, half + LANES), F32),
             pltpu.VMEM((7, 16, LANES), F32),
             pltpu.VMEM((wave_devices, 128, LANES), F32),
+            pltpu.SemaphoreType.DMA((2, STEPS)),
             pltpu.SemaphoreType.DMA((2,)),
             pltpu.SemaphoreType.DMA((2,)),
             pltpu.SemaphoreType.DMA((2,)),
@@ -519,23 +549,25 @@
             jax.ShapeDtypeStruct((slots, 5, 2, 2, pack), F32),
             jax.ShapeDtypeStruct((1, 2, 16, pad_len), F32),
         ),
-        grid=(slots // group,),
         in_specs=[
             smem,
             smem,
             smem,
-            whole(devices, 16, LANES),
-            whole(4, 32, table_len + LANES),
-            pl.BlockSpec((group, lat_pairs, pack), lambda s: (s, 0, 0)),
+            vmem,
+            vmem,
+            anywhere,
         ],
-        out_specs=(
-            pl.BlockSpec((group, 5, 2, 2, pack), lambda s: (s, 0, 0, 0, 0)),
-            whole(1, 2, 16, pad_len),
-        ),
+        out_specs=(anywhere, anywhere),
         scratch_shapes=[
+            pltpu.VMEM((slots, lat_pairs, pack), F32),
+            pltpu.VMEM((slots, 5, 2, 2, pack), F32),
+            pltpu.VMEM((1, 2, 16, pad_len), F32),
             pltpu.VMEM((LANES * 16, LANES), F32),
             pltpu.VMEM((slots * 40, LANES), F32),
             pltpu.VMEM((32, 4 * table_len), F32),
+            pltpu.SemaphoreType.DMA((1, STEPS)),
+            pltpu.SemaphoreType.DMA((1, STEPS)),
+            pltpu.SemaphoreType.DMA,
         ],
         compiler_params=pltpu.CompilerParams(vmem_limit_bytes=56 * MIB),
         name="direct",

time: 73.6 us -> 68.1 us (0.925)
  Pallas kernels: 71.1 us -> 66 us
    pallas_call x1, Pallas kernels: 14.4 us -> 10.6 us  [shards(): pl.pallas_call(functools.partial(direct_kernel, group), out_shape=(jax.Sh...]
    pallas_call x1, Pallas kernels: 56.7 us -> 55.4 us  [shards(): pl.pallas_call(functools.partial(main_kernel, group), out_shape=(jax.Shap...]
where the time goes in v4:
time: 68.1 us; the launch traced here: 67.9 us
  Pallas kernels  66 us (97%)
  local copies, waits for them, and re-layouts  1.27 us (2%)
    pallas_call x1, Pallas kernels, shards(): pl.pallas_call(functools.partial(main_kernel, group), out_shape=(jax.Shap...  55.4 us
    pallas_call x1, Pallas kernels, shards(): pl.pallas_call(functools.partial(direct_kernel, group), out_shape=(jax.Sh...  10.6 us

profile of v4, /device:TPU:1, one launch (start us, length us, event | category | flops | bytes accessed | tf_op | source)
XLA Modules:
  0.0 67.9 jit_solution(4048381670131305937)
XLA Ops:
  0.6 1.3 %broadcast_in_dim.3.map_ref = s32[1,640]{1,0:T(1,128)} reshape(s32[640]{0:T(1024)} %wave_ref.3) | data formatting | bytes 5120 | tf_op jit(solution)/shard_map/broadcast_in_dim | solution.py:544
  1.9 55.4 %rows.1 = (f32[4,32,1536]{2,1,0:T(8,128)}, f32[128,16,128]{2,1,0:T(8,128)}) custom-call(s32[640]{0:T(1024)} %wave_ref.3, s32[128]{0:T(128)} %band_ref.3, s32[64]{0:T(128)} %len_ref.3, f32[64]{0:T(128)} %gauss_ref.1, s32[1,640]{1,0:T(1,128)} %broadcast_in_dim.3.map_ref, f32[40,2,2,2,1281]{4,3,2,1,0:T(2,128)} %spec_hbm.1, f32[40,64,1281]{2,1,0:T(8,128)} %leg_hbm.3), custom_call_target="tpu_custom_call" | custom-call | tf_op jit(solution)/shard_map/rows/pallas_call | solution.py:492
  57.3 10.6 %direct.1 = (f32[40,5,2,2,1281]{4,3,2,1,0:T(2,128)}, f32[1,2,16,5248]{3,2,1,0:T(8,128)}) custom-call(s32[640]{0:T(1024)} %wave_ref.3, s32[128]{0:T(128)} %band_ref.3, s32[64]{0:T(128)} %len_ref.3, f32[128,16,128]{2,1,0:T(8,128)} %get-tuple-element.6.in_ref, f32[4,32,1536]{2,1,0:T(8,128)} %get-tuple-element.7.segs_ref, f32[40,64,1281]{2,1,0:T(8,128)} %leg_hbm.3), custom_call_target="tpu_custom_call" | custom-call | tf_op jit(solution)/shard_map/direct/pallas_call | solution.py:546

commit v5 on v4

--- a/solution.py
+++ b/solution.py
@@ -50,9 +50,12 @@
 
 
 def peer(k):
-    wave, level = lax.axis_index("wave"), lax.axis_index("level")
-    core, y, x, z = k % 2, k // 2 % 4, k // 8 % 4, k // 32
-    return (wave // 4 + z) % 4 * 4 + (wave % 4 + x) % 4, (level // 2 + y) % 4 * 2 + (level % 2 + core) % 2
+    mask = (k * 37) & 127
+    return lax.axis_index("wave") ^ (mask >> 3), lax.axis_index("level") ^ (mask & 7)
+
+
+def holder(place):
+    return (place & 3) * 4 + ((place + (place >> 2)) & 3)
 
 
 def send(source, target, sems, device):
@@ -127,10 +130,10 @@
 
 
 def main_kernel(
-    group, wave_ref, band_ref, len_ref, gauss_ref, map_ref, spec_hbm, leg_hbm, segs_ref, out_ref, spec_ref, leg_ref,
-    flat, sums, flat_rows, rows, row_ref, col_ref, send_ref, in_ref, sorted_x, even_x, odd_x, even_l, odd_l,
+    group, wave_ref, band_ref, len_ref, gauss_ref, map_hbm, spec_hbm, leg_hbm, segs_ref, out_ref, spec_ref, leg_ref,
+    flat, sums, flat_rows, rows, map_ref, mapped, row_ref, col_ref, send_ref, in_ref, sorted_x, even_x, odd_x, even_l, odd_l,
     even_hi, even_lo, odd_hi, odd_lo, segs, turned, even_f, odd_f, back, packed, back_ref,
-    load_sems, sems, back_sems, local_sems,
+    map_sems, load_sems, sems, back_sems, local_sems,
 ):
     devices = send_ref.shape[0]
     barrier = pltpu.get_barrier_semaphore()
@@ -138,6 +141,12 @@
     for n in range(STEPS):
         for copy in copies(n):
             copy.start()
+    map_copies = [
+        pltpu.make_async_copy(map_hbm.at[pl.ds(n * LANES, LANES)], map_ref.at[n], map_sems.at[n])
+        for n in range(map_ref.shape[0])
+    ]
+    for copy in map_copies:
+        copy.start()
     greeted = (devices - 1) // STEPS
 
     def greet(k):
@@ -154,16 +163,18 @@
     for k in range(STEPS * greeted + 1, devices):
         greet(k)
     sort_rows(band_ref, sums, flat_rows, rows, send_ref)
+    for copy in map_copies:
+        copy.wait()
     pl.semaphore_wait(barrier, devices - 1)
     row_part(
-        band_ref, len_ref, gauss_ref, map_ref, row_ref, col_ref, segs_ref, out_ref, send_ref, in_ref, sorted_x,
+        band_ref, len_ref, gauss_ref, map_ref, mapped, row_ref, col_ref, segs_ref, out_ref, send_ref, in_ref, sorted_x,
         even_x, odd_x, even_l, odd_l, even_hi, even_lo, odd_hi, odd_lo, segs, turned, even_f, odd_f, back, packed,
         back_ref, sems, back_sems, local_sems,
     )
 
 
 def row_part(
-    band_ref, len_ref, gauss_ref, map_ref, row_ref, col_ref, segs_ref, out_ref, send_ref, in_ref, sorted_x,
+    band_ref, len_ref, gauss_ref, map_ref, mapped, row_ref, col_ref, segs_ref, out_ref, send_ref, in_ref, sorted_x,
     even_x, odd_x, even_l, odd_l, even_hi, even_lo, odd_hi, odd_lo, segs, turned, even_f, odd_f, back, packed,
     back_ref, sems, back_sems, local_sems,
 ):
@@ -184,8 +195,12 @@
     tiles = even_hi.shape[1] // LANES
     lane = lax.broadcasted_iota(jnp.int32, (1, LANES), 1)
 
-    mapped = map_ref[...]
-    row_ref[...] = jnp.where((mapped & 1) == 0, mapped, wave_top - mapped)
+    for block in range(blocks):
+        mapped[:, block * LANES : (block + 1) * LANES] = map_ref[block : block + 1, :]
+    for place in range(devices):
+        begin = holder(place) * share
+        first = mapped[:, begin : begin + share]
+        row_ref[:, place * share : (place + 1) * share] = jnp.where((first & 1) == 0, first, wave_top - first)
     for block in range(blocks):
         at = slice(block * LANES, (block + 1) * LANES)
         col_ref[at, :] = jnp.broadcast_to(row_ref[:, at].astype(F32), (LANES, LANES)).T
@@ -238,7 +253,7 @@
         at = slice(dev * share, (dev + 1) * share)
         for j, units in enumerate(COEF_ROWS):
             for lv in range(2):
-                sorted_x[dev % 4, j, pl.ds(lv, 8, stride=2), :] = in_ref[dev, pl.ds(3 * lv + j, 8, stride=8), :]
+                sorted_x[dev % 4, j, pl.ds(lv, 8, stride=2), :] = in_ref[holder(dev), pl.ds(3 * lv + j, 8, stride=8), :]
             for n, (f, part, odd) in enumerate(units):
                 to = slice(32 * part + 16 * f, 32 * part + 16 * f + 16)
                 x_ref = odd_x if odd else even_x
@@ -321,10 +336,9 @@
         tiles_at = [pl.ds(pl.multiple_of((base + n) * LANES, LANES), LANES) for n in range(2)]
 
         def unit(x, odd, part, place):
-            to = place * share
-            shift = (to - offset + LANES) & (LANES - 1)
-            rolled = [pltpu.roll(back[2 * odd + part, 16 * x : 16 * x + 16, at], shift, 1) for at in tiles_at]
-            return jnp.where(lane - to + offset < LANES, rolled[0], rolled[1])
+            low, high = (back[2 * odd + part, 16 * x : 16 * x + 16, at] for at in tiles_at)
+            shift = (place * share - offset + LANES) & (LANES - 1)
+            return pltpu.roll(jnp.where(lane < offset, high, low), shift, 1)
 
         def joined(units):
             value = units[0]
@@ -344,14 +358,16 @@
                     ]
             back_ref[dev, pl.ds(12 + lv, 8, stride=16), :] = packed[6, pl.ds(lv, 8, stride=2), :]
 
+        to_wave = holder(dev)
+
         def start_block(to_level):
             block = back_ref.at[dev, pl.ds(pl.multiple_of(to_level * 16, 16), 14), :]
-            send(block, out_ref.at[here, pl.ds(0, 14), :], back_sems, (dev, to_level)).start()
+            send(block, out_ref.at[here, pl.ds(0, 14), :], back_sems, (to_wave, to_level)).start()
 
         for n in range(1, 8):
-            start_block((my_level + n) % levels)
-
-        @pl.when(dev != my_wave)
+            start_block(my_level ^ n)
+
+        @pl.when(to_wave != my_wave)
         def _():
             start_block(my_level)
 
@@ -372,8 +388,9 @@
         def _():
             send_back(3 * first)
 
+    my_place = ((my_wave - (my_wave >> 2)) & 3) * 4 + (my_wave >> 2)
     own_rows = pl.ds(pl.multiple_of(my_level * 16, 16), 16)
-    own = pltpu.make_async_copy(back_ref.at[my_wave, own_rows, :], out_ref.at[here], local_sems.at[1])
+    own = pltpu.make_async_copy(back_ref.at[my_place, own_rows, :], out_ref.at[here], local_sems.at[1])
     own.start()
 
     for i in range(4):
@@ -500,7 +517,7 @@
             smem,
             smem,
             smem,
-            vmem,
+            anywhere,
             anywhere,
             anywhere,
         ],
@@ -512,6 +529,8 @@
             pltpu.VMEM((slots * 32, LANES), F32),
             pltpu.VMEM((LANES * 8, LANES), F32),
             pltpu.VMEM((LANES, 8, LANES), F32),
+            pltpu.VMEM((half // LANES, LANES), jnp.int32),
+            pltpu.VMEM((1, half), jnp.int32),
             pltpu.VMEM((1, half), jnp.int32),
             pltpu.VMEM((half, LANES), F32),
             pltpu.VMEM((devices, 8, LANES), F32),
@@ -532,6 +551,7 @@
             pltpu.VMEM((4, 80, half + LANES), F32),
             pltpu.VMEM((7, 16, LANES), F32),
             pltpu.VMEM((wave_devices, 128, LANES), F32),
+            pltpu.SemaphoreType.DMA((half // LANES,)),
             pltpu.SemaphoreType.DMA((2, STEPS)),
             pltpu.SemaphoreType.DMA((2,)),
             pltpu.SemaphoreType.DMA((2,)),
@@ -541,7 +561,7 @@
             collective_id=0, has_side_effects=True, vmem_limit_bytes=56 * MIB
         ),
         name="rows",
-    )(wave_map, band_map, row_len, gauss, wave_map[None, :], spec_in, legendre)
+    )(wave_map, band_map, row_len, gauss, wave_map, spec_in, legendre)
 
     spec_out, grid_out = pl.pallas_call(
         functools.partial(direct_kernel, group),

time: 68.1 us -> 62.3 us (0.915)
  Pallas kernels: 66 us -> 61.5 us
  local copies, waits for them, and re-layouts: 1.27 us -> 0 us
    pallas_call x1, Pallas kernels: 55.4 us -> 50.9 us  [shards(): pl.pallas_call(functools.partial(main_kernel, group), out_shape=(jax.Shap...]
    broadcast_in_dim x1 -> x0, local copies, waits for them, and re-layouts: 1.27 us -> none  [shards(): wave_map[None, :]]
where the time goes in v5:
time: 62.3 us; the launch traced here: 62.2 us
  Pallas kernels  61.5 us (99%)
  between operations  0.64 us (1%)
    pallas_call x1, Pallas kernels, shards(): pl.pallas_call(functools.partial(main_kernel, group), out_shape=(jax.Shap...  50.9 us
    pallas_call x1, Pallas kernels, shards(): pl.pallas_call(functools.partial(direct_kernel, group), out_shape=(jax.Sh...  10.6 us

profile of v5, /device:TPU:1, one launch (start us, length us, event | category | flops | bytes accessed | tf_op | source)
XLA Modules:
  0.0 62.2 jit_solution(12733727897065971060)
XLA Ops:
  0.6 50.9 %rows.1 = (f32[4,32,1536]{2,1,0:T(8,128)}, f32[128,16,128]{2,1,0:T(8,128)}) custom-call(s32[640]{0:T(1024)} %wave_ref.3, s32[128]{0:T(128)} %band_ref.3, s32[64]{0:T(128)} %len_ref.3, f32[64]{0:T(128)} %gauss_ref.1, s32[640]{0:T(1024)} %wave_ref.3, f32[40,2,2,2,1281]{4,3,2,1,0:T(2,128)} %spec_hbm.1, f32[40,64,1281]{2,1,0:T(8,128)} %leg_hbm.3), custom_call_target="tpu_custom_call" | custom-call | tf_op jit(solution)/shard_map/rows/pallas_call | solution.py:509
  51.6 10.6 %direct.1 = (f32[40,5,2,2,1281]{4,3,2,1,0:T(2,128)}, f32[1,2,16,5248]{3,2,1,0:T(8,128)}) custom-call(s32[640]{0:T(1024)} %wave_ref.3, s32[128]{0:T(128)} %band_ref.3, s32[64]{0:T(128)} %len_ref.3, f32[128,16,128]{2,1,0:T(8,128)} %get-tuple-element.6.in_ref, f32[4,32,1536]{2,1,0:T(8,128)} %get-tuple-element.7.segs_ref, f32[40,64,1281]{2,1,0:T(8,128)} %leg_hbm.3), custom_call_target="tpu_custom_call" | custom-call | tf_op jit(solution)/shard_map/direct/pallas_call | solution.py:566

commit v6 on v5

--- a/solution.py
+++ b/solution.py
@@ -12,7 +12,9 @@
 BF16 = jnp.bfloat16
 LANES = 128
 MIB = 1 << 20
-STEPS = 10
+INVERSE_STEPS = 4
+DIRECT_STEPS = 5
+TOGETHER = 2
 SIN_TERMS = [(-1.0) ** i / math.factorial(2 * i + 1) for i in range(6)]
 COS_TERMS = [(-1.0) ** i / math.factorial(2 * i) for i in range(7)]
 MESH = pl.DeviceIdType.MESH
@@ -64,6 +66,11 @@
     )
 
 
+def chunks_of(pack):
+    ends = list(range(256, pack - 255, 256)) + [pack]
+    return list(zip([0] + ends[:-1], ends))
+
+
 def group_copies(group, sources, targets, sems):
     def copies(n):
         at = pl.ds(n * group, group)
@@ -79,28 +86,37 @@
     slots = sums.shape[0] // 32
     pack = leg_ref.shape[2]
     wave_pos = lax.axis_index("wave")
-    position = lax.broadcasted_iota(jnp.int32, (8, pack), 1)
     for g in range(group):
-        slot = step * group + g
-        first_wave = wave_ref[wave_pos * slots + slot]
-        boundary = (pack - 1) - first_wave
         for pair in range(4):
-            flat[g, 2 * pair : 2 * pair + 2, :] = spec_ref[slot, pair // 2, pair % 2]
-        x = flat[g]
-        in_first = position < boundary
-        parity = jnp.where(in_first, position, position + boundary) & 1
-        in_even = in_first == ((first_wave & 1) == 0)
-        high = x.astype(BF16).astype(F32)
-        parts = []
-        for part in (high, x - high):
-            signed = jnp.where(parity == 0, part, -part)
-            for kept in (in_even, jnp.logical_not(in_even)):
-                parts += [jnp.where(kept, part, 0.0), jnp.where(kept, signed, 0.0)]
-        left = jnp.concatenate(parts, axis=0).astype(BF16)
-        right = jnp.concatenate(split(leg_ref[slot]), axis=0)
-        both = dot(left, right, NT)
-        both = both[:32] + both[32:]
-        sums[pl.ds(pl.multiple_of(slot * 32, 32), 32), :] = both + pltpu.roll(both, 64, 1)
+            flat[g, 2 * pair : 2 * pair + 2, :] = spec_ref[step * group + g, pair // 2, pair % 2]
+    results = []
+    for g in range(0, group, TOGETHER):
+        both = None
+        for begin, end in chunks_of(pack):
+            at = slice(begin, end)
+            position = begin + lax.broadcasted_iota(jnp.int32, (8, end - begin), 1)
+            parts, tables = [], []
+            for n in range(g, g + TOGETHER):
+                first_wave = wave_ref[wave_pos * slots + step * group + n]
+                boundary = (pack - 1) - first_wave
+                in_first = position < boundary
+                parity = jnp.where(in_first, position, position + boundary) & 1
+                in_even = in_first == ((first_wave & 1) == 0)
+                x = flat[n, :, at]
+                high = x.astype(BF16).astype(F32)
+                for part in (high, x - high):
+                    signed = jnp.where(parity == 0, part, -part)
+                    for kept in (in_even, jnp.logical_not(in_even)):
+                        parts += [jnp.where(kept, part, 0.0), jnp.where(kept, signed, 0.0)]
+                tables += split(leg_ref[step * group + n, :, at])
+            left = jnp.concatenate(parts, axis=0).astype(BF16)
+            product = dot(left, jnp.concatenate(tables, axis=0), NT)
+            both = product if both is None else both + product
+        for n in range(TOGETHER):
+            own = both[64 * n : 64 * n + 64, LANES * n : LANES * n + LANES]
+            own = own[:32] + own[32:]
+            results.append(own + pltpu.roll(own, 64, 1))
+    sums[pl.ds(pl.multiple_of(step * (32 * group), 32), 32 * group), :] = jnp.concatenate(results, axis=0)
 
 
 def sort_rows(band_ref, sums, flat_rows, rows, out_ref):
@@ -138,7 +154,7 @@
     devices = send_ref.shape[0]
     barrier = pltpu.get_barrier_semaphore()
     copies = group_copies(group, (spec_hbm, leg_hbm), (spec_ref, leg_ref), load_sems)
-    for n in range(STEPS):
+    for n in range(INVERSE_STEPS):
         for copy in copies(n):
             copy.start()
     map_copies = [
@@ -147,21 +163,22 @@
     ]
     for copy in map_copies:
         copy.start()
-    greeted = (devices - 1) // STEPS
 
     def greet(k):
         pl.semaphore_signal(barrier, inc=1, device_id=peer(k), device_id_type=MESH)
 
-    @pl.loop(0, STEPS)
+    greet(1)
+
+    @pl.loop(2, devices, unroll=14)
+    def _(k):
+        greet(k)
+
+    @pl.loop(0, INVERSE_STEPS)
     def _(step):
         for copy in copies(step):
             copy.wait()
-        for n in range(greeted):
-            greet(step * greeted + n + 1)
         inverse_step(step, group, wave_ref, spec_ref, leg_ref, flat, sums)
 
-    for k in range(STEPS * greeted + 1, devices):
-        greet(k)
     sort_rows(band_ref, sums, flat_rows, rows, send_ref)
     for copy in map_copies:
         copy.wait()
@@ -260,8 +277,9 @@
                 x_ref[to, at] = sorted_x[dev % 4, j, :, n * share : (n + 1) * share]
 
     highest = jnp.minimum(wave_top, lax.shift_right_logical(length - 1, 1))
-    for block in range(blocks):
-        at = slice(block * LANES, (block + 1) * LANES)
+    @pl.loop(0, blocks)
+    def _(block):
+        at = pl.ds(pl.multiple_of(block * LANES, LANES), LANES)
         evens = row_ref[:, at]
         for odd, x_ref, l_ref in ((False, even_x, even_l), (True, odd_x, odd_l)):
             wave = wave_top - evens if odd else evens
@@ -279,21 +297,18 @@
                 on_cos = jnp.concatenate([a, flip * a], axis=0)
                 on_sin = jnp.concatenate([-b, -flip * b], axis=0)
             for offset, value in ((0, on_cos), (LANES, on_sin)):
-                to = slice(block * 256 + offset, block * 256 + offset + LANES)
+                to = pl.ds(pl.multiple_of(block * 256 + offset, LANES), LANES)
                 high, low = split(value)
                 l_ref[0:128, to] = high
                 l_ref[128:256, to] = low
 
-    start = 0
-    while start < tiles * LANES:
-        width = min(256, tiles * LANES - start)
-        at = slice(start, start + width)
-        start += width
+    def grid_values(start, width):
+        at = pl.ds(pl.multiple_of(start, LANES), width)
         halves = []
         for l_ref, table_hi, table_lo in ((even_l, even_hi, even_lo), (odd_l, odd_hi, odd_lo)):
             whole = dot(l_ref[...], table_hi[:, at], NN)
             halves.append(whole[:128] + whole[128:] + dot(l_ref[0:128, :], table_lo[:, at], NN))
-        inside = (at.start + lax.broadcasted_iota(jnp.int32, (1, width), 1)) < quarter
+        inside = (start + lax.broadcasted_iota(jnp.int32, (1, width), 1)) < quarter
         even, odd = (jnp.where(inside, half, 0.0) for half in halves)
         quarters = [even[:64] + odd[:64], even[64:] - odd[64:], even[:64] - odd[:64], even[64:] + odd[64:]]
         fluxes = []
@@ -307,6 +322,13 @@
                 high, low = split(value)
                 f_ref[80 * n : 80 * n + 80, at] = high
                 f_ref[160 + 80 * n : 240 + 80 * n, at] = low
+
+    @pl.loop(0, tiles // 2)
+    def _(pair):
+        grid_values(pair * 256, 256)
+
+    if tiles % 2:
+        grid_values((tiles - 1) * LANES, LANES)
 
     scale = gauss_ref[row] * inverse
 
@@ -380,20 +402,19 @@
         low = jnp.where((turn == 0) & (block > 0), 3 * block + 1, 3 * block)
         high = jnp.where(block == blocks - 1, devices, 3 * block + 3)
 
-        @pl.loop(low, high)
-        def _(dev):
-            send_back(dev)
-
-        @pl.when((turn == blocks - 1) & (first > 0))
-        def _():
-            send_back(3 * first)
+        extra = jnp.where((turn == blocks - 1) & (first > 0), 1, 0)
+
+        @pl.loop(low, high + extra)
+        def _(n):
+            send_back(jnp.where(n == high, 3 * first, n))
 
     my_place = ((my_wave - (my_wave >> 2)) & 3) * 4 + (my_wave >> 2)
     own_rows = pl.ds(pl.multiple_of(my_level * 16, 16), 16)
     own = pltpu.make_async_copy(back_ref.at[my_place, own_rows, :], out_ref.at[here], local_sems.at[1])
     own.start()
 
-    for i in range(4):
+    @pl.loop(0, 4)
+    def _(i):
         shift = (i * quarter) & (LANES - 1)
         before = jnp.zeros((32, LANES), F32)
         for tile in range(tiles + 1):
@@ -401,6 +422,7 @@
             rolled = pltpu.roll(segs[i, :, at], shift, 1) if tile < tiles else jnp.zeros((32, LANES), F32)
             turned[i, :, at] = jnp.where(lane < shift, before, rolled)
             before = rolled
+
     grid_copy = pltpu.make_async_copy(turned, segs_ref, local_sems.at[0])
     grid_copy.start()
 
@@ -430,11 +452,11 @@
     leg_ref, spec_ref, grid_ref, natural, turned, acc, load_sems, store_sems, grid_sem,
 ):
     pack = leg_ref.shape[2]
-    slots = STEPS * group
+    slots = DIRECT_STEPS * group
     wave_pos = lax.axis_index("wave")
     loads = group_copies(group, (leg_hbm,), (leg_ref,), load_sems)
     stores = group_copies(group, (spec_ref,), (spec_hbm,), store_sems)
-    for n in range(STEPS):
+    for n in range(DIRECT_STEPS):
         loads(n)[0].start()
 
     @pl.loop(0, in_ref.shape[0], unroll=8)
@@ -447,46 +469,64 @@
             block = natural[pl.ds(line, LANES, stride=16), :].T
             placed = [(x, odd, part) for x, odd in units] or [(4, 1, 0), (4, 1, 1)]
             for n, (x, odd, p) in enumerate(placed):
-                to = 4 * x + 2 * lv + p + (16 if x < 4 else 4) * odd + (16 if x == 4 else 0)
-                turned[pl.ds(to, slots, stride=40), :] = block[n * slots : (n + 1) * slots]
+                to = 4 * x + 2 * lv + p + 24 * odd
+                turned[pl.ds(to, slots, stride=48), :] = block[n * slots : (n + 1) * slots]
 
     row = band_ref[wave_pos * lax.axis_size("level") + lax.axis_index("level")] & 63
     lay_quarters(lax.shift_right_logical(len_ref[row], 2), segs_ref, acc, grid_ref)
     grid_copy = pltpu.make_async_copy(grid_ref, grid_hbm, grid_sem)
     grid_copy.start()
 
-    position = lax.broadcasted_iota(jnp.int32, (1, pack), 1)
     south = lax.broadcasted_iota(jnp.int32, (1, LANES), 1) >= 64
 
-    @pl.loop(0, STEPS)
+    def both_parities(x):
+        other = pltpu.roll(x, 64, 1)
+        difference = x - other
+        y = jnp.concatenate([x + other, jnp.where(south, -difference, difference)], axis=0)
+        return jnp.concatenate(split(y), axis=0)
+
+    def store_chunk(both, slot, boundary, begin, end):
+        position = begin + lax.broadcasted_iota(jnp.int32, (1, end - begin), 1)
+        rows = both.shape[0] // 2
+        both = both[:rows] + both[rows:]
+        if end <= pack // 2:
+            chosen = jnp.where((position & 1) == 0, both[:24], both[24:])
+            main, last = chosen[:16], chosen[16:20]
+        else:
+            in_first = position < boundary
+            parity = jnp.where(in_first, position, position + boundary) & 1
+            chosen = jnp.where(parity == 0, both[:40], both[40:])
+            main = jnp.where(in_first, chosen[:16], chosen[16:32])
+            last = jnp.where(in_first, chosen[32:36], chosen[36:40])
+        for n in range(10):
+            value = main[2 * n : 2 * n + 2] if n < 8 else last[2 * n - 16 : 2 * n - 14]
+            spec_ref[slot, n // 2, n % 2, :, begin:end] = value
+
+    @pl.loop(0, DIRECT_STEPS)
     def _(step):
         loads(step)[0].wait()
+        stored = None
         for g in range(group):
             slot = step * group + g
             first_wave = wave_ref[wave_pos * slots + slot]
             boundary = (pack - 1) - first_wave
-
-            x = turned[pl.ds(pl.multiple_of(slot * 40, 8), 40), :]
-            other = pltpu.roll(x, 64, 1)
-            difference = x - other
-            y = jnp.concatenate([x + other, jnp.where(south, -difference, difference)], axis=0)
-            left = jnp.concatenate(split(y), axis=0)
-            right = jnp.concatenate(split(leg_ref[slot]), axis=0)
-            both = dot(left, right, NN)
-            both = both[:80] + both[80:]
-            in_first = position < boundary
-            parity = jnp.where(in_first, position, position + boundary) & 1
-            in_even = in_first == ((first_wave & 1) == 0)
-            chosen = jnp.where(parity == 0, both[:40], both[40:])
-            main = jnp.where(in_even, chosen[:16], chosen[16:32])
-            last = jnp.where(in_even, chosen[32:36], chosen[36:40])
-            for n in range(8):
-                spec_ref[slot, n // 2, n % 2] = main[2 * n : 2 * n + 2]
-            for n in range(2):
-                spec_ref[slot, 4, n] = last[2 * n : 2 * n + 2]
+            first_at = slot * 48 + (first_wave & 1) * 24
+            x = turned[pl.ds(pl.multiple_of(first_at, 8), 24), :]
+            second_x = turned[pl.ds(pl.multiple_of(slot * 96 + 24 - first_at, 8), 24), :]
+            last = jnp.concatenate([x[16:20], second_x[16:20]], axis=0)
+            first_left = both_parities(x)
+            left = both_parities(jnp.concatenate([x[:16], second_x[:16], last], axis=0))
+            for begin, end in chunks_of(pack):
+                at = slice(begin, end)
+                right = jnp.concatenate(split(leg_ref[slot, :, at]), axis=0)
+                both = dot(first_left if end <= pack // 2 else left, right, NN)
+                if stored is not None:
+                    store_chunk(*stored)
+                stored = (both, slot, boundary, begin, end)
+        store_chunk(*stored)
         stores(step)[0].start()
 
-    for n in range(STEPS):
+    for n in range(DIRECT_STEPS):
         stores(n)[0].wait()
     grid_copy.wait()
 
@@ -500,7 +540,7 @@
     pad_len = (20 + 4 * (waves - 1) + 127) // 128 * 128
     table_len = (pad_len // 4 + 127) // 128 * 128
     smem = pl.BlockSpec(memory_space=pltpu.SMEM)
-    group = slots // STEPS
+    group = slots // INVERSE_STEPS
 
     vmem = pl.BlockSpec(memory_space=pltpu.VMEM)
     anywhere = pl.BlockSpec(memory_space=pl.ANY)
@@ -552,7 +592,7 @@
             pltpu.VMEM((7, 16, LANES), F32),
             pltpu.VMEM((wave_devices, 128, LANES), F32),
             pltpu.SemaphoreType.DMA((half // LANES,)),
-            pltpu.SemaphoreType.DMA((2, STEPS)),
+            pltpu.SemaphoreType.DMA((2, INVERSE_STEPS)),
             pltpu.SemaphoreType.DMA((2,)),
             pltpu.SemaphoreType.DMA((2,)),
             pltpu.SemaphoreType.DMA((2,)),
@@ -564,7 +604,7 @@
     )(wave_map, band_map, row_len, gauss, wave_map, spec_in, legendre)
 
     spec_out, grid_out = pl.pallas_call(
-        functools.partial(direct_kernel, group),
+        functools.partial(direct_kernel, slots // DIRECT_STEPS),
         out_shape=(
             jax.ShapeDtypeStruct((slots, 5, 2, 2, pack), F32),
             jax.ShapeDtypeStruct((1, 2, 16, pad_len), F32),
@@ -583,10 +623,10 @@
             pltpu.VMEM((slots, 5, 2, 2, pack), F32),
             pltpu.VMEM((1, 2, 16, pad_len), F32),
             pltpu.VMEM((LANES * 16, LANES), F32),
-            pltpu.VMEM((slots * 40, LANES), F32),
+            pltpu.VMEM((slots * 48, LANES), F32),
             pltpu.VMEM((32, 4 * table_len), F32),
-            pltpu.SemaphoreType.DMA((1, STEPS)),
-            pltpu.SemaphoreType.DMA((1, STEPS)),
+            pltpu.SemaphoreType.DMA((1, DIRECT_STEPS)),
+            pltpu.SemaphoreType.DMA((1, DIRECT_STEPS)),
             pltpu.SemaphoreType.DMA,
         ],
         compiler_params=pltpu.CompilerParams(vmem_limit_bytes=56 * MIB),

time: 62.3 us -> 58.5 us (0.939)
  the two profiles are of different devices: /device:TPU:1 before, /device:TPU:33 now
where the time goes in v6:
time: 58.5 us; the launch traced here: 58.3 us
  Pallas kernels  57.7 us (99%)
  between operations  0.64 us (1%)
    pallas_call x1, Pallas kernels, shards(): pl.pallas_call(functools.partial(main_kernel, group), out_shape=(jax.Shap...  48 us
    pallas_call x1, Pallas kernels, shards(): pl.pallas_call(functools.partial(direct_kernel, slots // DIRECT_STEPS), o...  9.7 us

profile of v6, /device:TPU:33, one launch (start us, length us, event | category | flops | bytes accessed | tf_op | source)
XLA Modules:
  0.0 58.3 jit_solution(2180859851180360131)
XLA Ops:
  0.6 48.0 %rows.1 = (f32[4,32,1536]{2,1,0:T(8,128)}, f32[128,16,128]{2,1,0:T(8,128)}) custom-call(s32[640]{0:T(1024)} %wave_ref.3, s32[128]{0:T(128)} %band_ref.3, s32[64]{0:T(128)} %len_ref.3, f32[64]{0:T(128)} %gauss_ref.1, s32[640]{0:T(1024)} %wave_ref.3, f32[40,2,2,2,1281]{4,3,2,1,0:T(2,128)} %spec_hbm.1, f32[40,64,1281]{2,1,0:T(8,128)} %leg_hbm.3), custom_call_target="tpu_custom_call" | custom-call | tf_op jit(solution)/shard_map/rows/pallas_call | solution.py:549
  48.6 9.7 %direct.1 = (f32[40,5,2,2,1281]{4,3,2,1,0:T(2,128)}, f32[1,2,16,5248]{3,2,1,0:T(8,128)}) custom-call(s32[640]{0:T(1024)} %wave_ref.3, s32[128]{0:T(128)} %band_ref.3, s32[64]{0:T(128)} %len_ref.3, f32[128,16,128]{2,1,0:T(8,128)} %get-tuple-element.6.in_ref, f32[4,32,1536]{2,1,0:T(8,128)} %get-tuple-element.7.segs_ref, f32[40,64,1281]{2,1,0:T(8,128)} %leg_hbm.3), custom_call_target="tpu_custom_call" | custom-call | tf_op jit(solution)/shard_map/direct/pallas_call | solution.py:606

commit v7 on v6

--- a/solution.py
+++ b/solution.py
@@ -14,6 +14,7 @@
 MIB = 1 << 20
 INVERSE_STEPS = 4
 DIRECT_STEPS = 5
+AHEAD = 2
 TOGETHER = 2
 SIN_TERMS = [(-1.0) ** i / math.factorial(2 * i + 1) for i in range(6)]
 COS_TERMS = [(-1.0) ** i / math.factorial(2 * i) for i in range(7)]
@@ -80,6 +81,13 @@
         ]
 
     return copies
+
+
+def small_copies(sources, targets, sems):
+    return [
+        pltpu.make_async_copy(source, target, sems.at[i])
+        for i, (source, target) in enumerate(zip(sources, targets))
+    ]
 
 
 def inverse_step(step, group, wave_ref, spec_ref, leg_ref, flat, sums):
@@ -146,10 +154,11 @@
 
 
 def main_kernel(
-    group, wave_ref, band_ref, len_ref, gauss_ref, map_hbm, spec_hbm, leg_hbm, segs_ref, out_ref, spec_ref, leg_ref,
+    group, wave_hbm, band_hbm, len_hbm, gauss_hbm, spec_hbm, leg_hbm, segs_ref, out_ref,
+    wave_ref, band_ref, len_ref, gauss_ref, spec_ref, leg_ref,
     flat, sums, flat_rows, rows, map_ref, mapped, row_ref, col_ref, send_ref, in_ref, sorted_x, even_x, odd_x, even_l, odd_l,
     even_hi, even_lo, odd_hi, odd_lo, segs, turned, even_f, odd_f, back, packed, back_ref,
-    map_sems, load_sems, sems, back_sems, local_sems,
+    small_sems, map_sems, load_sems, sems, back_sems, local_sems,
 ):
     devices = send_ref.shape[0]
     barrier = pltpu.get_barrier_semaphore()
@@ -158,10 +167,13 @@
         for copy in copies(n):
             copy.start()
     map_copies = [
-        pltpu.make_async_copy(map_hbm.at[pl.ds(n * LANES, LANES)], map_ref.at[n], map_sems.at[n])
+        pltpu.make_async_copy(wave_hbm.at[pl.ds(n * LANES, LANES)], map_ref.at[n], map_sems.at[n])
         for n in range(map_ref.shape[0])
     ]
-    for copy in map_copies:
+    small = small_copies(
+        (wave_hbm, band_hbm, len_hbm, gauss_hbm), (wave_ref, band_ref, len_ref, gauss_ref), small_sems
+    )
+    for copy in map_copies + small:
         copy.start()
 
     def greet(k):
@@ -172,6 +184,9 @@
     @pl.loop(2, devices, unroll=14)
     def _(k):
         greet(k)
+
+    for copy in small:
+        copy.wait()
 
     @pl.loop(0, INVERSE_STEPS)
     def _(step):
@@ -448,16 +463,23 @@
 
 
 def direct_kernel(
-    group, wave_ref, band_ref, len_ref, in_ref, segs_ref, leg_hbm, spec_hbm, grid_hbm,
-    leg_ref, spec_ref, grid_ref, natural, turned, acc, load_sems, store_sems, grid_sem,
+    group, wave_hbm, band_hbm, len_hbm, in_hbm, segs_hbm, leg_hbm, spec_hbm, grid_hbm,
+    wave_ref, band_ref, len_ref, in_ref, segs_ref, leg_ref, spec_ref, grid_ref, natural, turned, acc, small_sems, load_sems, store_sems, grid_sem,
 ):
     pack = leg_ref.shape[2]
     slots = DIRECT_STEPS * group
     wave_pos = lax.axis_index("wave")
     loads = group_copies(group, (leg_hbm,), (leg_ref,), load_sems)
     stores = group_copies(group, (spec_ref,), (spec_hbm,), store_sems)
-    for n in range(DIRECT_STEPS):
-        loads(n)[0].start()
+    small = small_copies(
+        (wave_hbm, band_hbm, len_hbm, in_hbm, segs_hbm), (wave_ref, band_ref, len_ref, in_ref, segs_ref), small_sems
+    )
+    for copy in small[:4] + loads(0):
+        copy.start()
+    for copy in small[:4]:
+        copy.wait()
+    for copy in small[4:] + loads(1):
+        copy.start()
 
     @pl.loop(0, in_ref.shape[0], unroll=8)
     def _(i):
@@ -472,6 +494,7 @@
                 to = 4 * x + 2 * lv + p + 24 * odd
                 turned[pl.ds(to, slots, stride=48), :] = block[n * slots : (n + 1) * slots]
 
+    small[4].wait()
     row = band_ref[wave_pos * lax.axis_size("level") + lax.axis_index("level")] & 63
     lay_quarters(lax.shift_right_logical(len_ref[row], 2), segs_ref, acc, grid_ref)
     grid_copy = pltpu.make_async_copy(grid_ref, grid_hbm, grid_sem)
@@ -505,6 +528,11 @@
     @pl.loop(0, DIRECT_STEPS)
     def _(step):
         loads(step)[0].wait()
+
+        @pl.when(step < DIRECT_STEPS - AHEAD)
+        def _():
+            loads(step + AHEAD)[0].start()
+
         stored = None
         for g in range(group):
             slot = step * group + g
@@ -539,10 +567,8 @@
     lat_pairs = legendre.shape[1]
     pad_len = (20 + 4 * (waves - 1) + 127) // 128 * 128
     table_len = (pad_len // 4 + 127) // 128 * 128
-    smem = pl.BlockSpec(memory_space=pltpu.SMEM)
     group = slots // INVERSE_STEPS
 
-    vmem = pl.BlockSpec(memory_space=pltpu.VMEM)
     anywhere = pl.BlockSpec(memory_space=pl.ANY)
     half = waves // 2
     table = pltpu.VMEM((waves, table_len), BF16)
@@ -552,17 +578,13 @@
             jax.ShapeDtypeStruct((4, 32, table_len + LANES), F32),
             jax.ShapeDtypeStruct((devices, 16, LANES), F32),
         ),
-        in_specs=[
-            smem,
-            smem,
-            smem,
-            smem,
-            anywhere,
-            anywhere,
-            anywhere,
-        ],
+        in_specs=[anywhere] * 6,
         out_specs=(anywhere, anywhere),
         scratch_shapes=[
+            pltpu.SMEM((waves // 2,), jnp.int32),
+            pltpu.SMEM((devices,), jnp.int32),
+            pltpu.SMEM((lat_pairs,), jnp.int32),
+            pltpu.SMEM((lat_pairs,), F32),
             pltpu.VMEM((slots, 2, 2, 2, pack), F32),
             pltpu.VMEM((slots, lat_pairs, pack), F32),
             pltpu.VMEM((group, 8, pack), F32),
@@ -591,6 +613,7 @@
             pltpu.VMEM((4, 80, half + LANES), F32),
             pltpu.VMEM((7, 16, LANES), F32),
             pltpu.VMEM((wave_devices, 128, LANES), F32),
+            pltpu.SemaphoreType.DMA((4,)),
             pltpu.SemaphoreType.DMA((half // LANES,)),
             pltpu.SemaphoreType.DMA((2, INVERSE_STEPS)),
             pltpu.SemaphoreType.DMA((2,)),
@@ -601,7 +624,7 @@
             collective_id=0, has_side_effects=True, vmem_limit_bytes=56 * MIB
         ),
         name="rows",
-    )(wave_map, band_map, row_len, gauss, wave_map, spec_in, legendre)
+    )(wave_map, band_map, row_len, gauss, spec_in, legendre)
 
     spec_out, grid_out = pl.pallas_call(
         functools.partial(direct_kernel, slots // DIRECT_STEPS),
@@ -609,22 +632,21 @@
             jax.ShapeDtypeStruct((slots, 5, 2, 2, pack), F32),
             jax.ShapeDtypeStruct((1, 2, 16, pad_len), F32),
         ),
-        in_specs=[
-            smem,
-            smem,
-            smem,
-            vmem,
-            vmem,
-            anywhere,
-        ],
+        in_specs=[anywhere] * 6,
         out_specs=(anywhere, anywhere),
         scratch_shapes=[
+            pltpu.SMEM((waves // 2,), jnp.int32),
+            pltpu.SMEM((devices,), jnp.int32),
+            pltpu.SMEM((lat_pairs,), jnp.int32),
+            pltpu.VMEM((devices, 16, LANES), F32),
+            pltpu.VMEM((4, 32, table_len + LANES), F32),
             pltpu.VMEM((slots, lat_pairs, pack), F32),
             pltpu.VMEM((slots, 5, 2, 2, pack), F32),
             pltpu.VMEM((1, 2, 16, pad_len), F32),
             pltpu.VMEM((LANES * 16, LANES), F32),
             pltpu.VMEM((slots * 48, LANES), F32),
             pltpu.VMEM((32, 4 * table_len), F32),
+            pltpu.SemaphoreType.DMA((5,)),
             pltpu.SemaphoreType.DMA((1, DIRECT_STEPS)),
             pltpu.SemaphoreType.DMA((1, DIRECT_STEPS)),
             pltpu.SemaphoreType.DMA,

time: 58.5 us -> 57.1 us (0.976)
  the two profiles are of different devices: /device:TPU:33 before, /device:TPU:32 now
where the time goes in v7:
time: 57.1 us; the launch traced here: 57 us
  Pallas kernels  56.4 us (99%)
  between operations  0.64 us (1%)
    pallas_call x1, Pallas kernels, shards(): pl.pallas_call(functools.partial(main_kernel, group), out_shape=(jax.Shap...  46.7 us
    pallas_call x1, Pallas kernels, shards(): pl.pallas_call(functools.partial(direct_kernel, slots // DIRECT_STEPS), o...  9.62 us

profile of v7, /device:TPU:32, one launch (start us, length us, event | category | flops | bytes accessed | tf_op | source)
XLA Modules:
  0.0 57.0 jit_solution(8865766607438454780)
XLA Ops:
  0.6 46.7 %rows.1 = (f32[4,32,1536]{2,1,0:T(8,128)}, f32[128,16,128]{2,1,0:T(8,128)}) custom-call(s32[640]{0:T(1024)} %wave_hbm.3, s32[128]{0:T(128)} %band_hbm.3, s32[64]{0:T(128)} %len_hbm.3, f32[64]{0:T(128)} %gauss_hbm.1, f32[40,2,2,2,1281]{4,3,2,1,0:T(2,128)} %spec_hbm.1, f32[40,64,1281]{2,1,0:T(8,128)} %leg_hbm.3), custom_call_target="tpu_custom_call" | custom-call | tf_op jit(solution)/shard_map/rows/pallas_call | solution.py:575
  47.4 9.6 %direct.1 = (f32[40,5,2,2,1281]{4,3,2,1,0:T(2,128)}, f32[1,2,16,5248]{3,2,1,0:T(8,128)}) custom-call(s32[640]{0:T(1024)} %wave_hbm.3, s32[128]{0:T(128)} %band_hbm.3, s32[64]{0:T(128)} %len_hbm.3, f32[128,16,128]{2,1,0:T(8,128)} %get-tuple-element.6.in_hbm, f32[4,32,1536]{2,1,0:T(8,128)} %get-tuple-element.7.segs_hbm, f32[40,64,1281]{2,1,0:T(8,128)} %leg_hbm.3), custom_call_target="tpu_custom_call" | custom-call | tf_op jit(solution)/shard_map/direct/pallas_call | solution.py:629

commit v8 on v7

--- a/solution.py
+++ b/solution.py
@@ -651,7 +651,7 @@
             pltpu.SemaphoreType.DMA((1, DIRECT_STEPS)),
             pltpu.SemaphoreType.DMA,
         ],
-        compiler_params=pltpu.CompilerParams(vmem_limit_bytes=56 * MIB),
+        compiler_params=pltpu.CompilerParams(vmem_limit_bytes=50 * MIB),
         name="direct",
     )(wave_map, band_map, row_len, returned, segs, legendre)
     return (grid_out, spec_out)

time: 57.1 us -> 59.5 us (1.042)
  the two profiles are of different devices: /device:TPU:32 before, /device:TPU:33 now
where the time goes in v8:
time: 59.5 us; the launch traced here: 59.3 us
  Pallas kernels  56.2 us (94%)
  local copies, waits for them, and re-layouts  2.36 us (4%)
  between operations  0.7 us (1%)
    pallas_call x1, Pallas kernels, shards(): pl.pallas_call(functools.partial(main_kernel, group), out_shape=(jax.Shap...  47.3 us
    pallas_call x1, Pallas kernels, shards(): pl.pallas_call(functools.partial(direct_kernel, slots // DIRECT_STEPS), o...  8.9 us
    unnamed x10, local copies, waits for them, and re-layouts  2.36 us

profile of v8, /device:TPU:33, one launch (start us, length us, event | category | flops | bytes accessed | tf_op | source)
XLA Modules:
  0.0 59.3 jit_solution(3253327326044138707)
XLA Ops:
  0.6 0.0 copy-start.4
  0.6 0.0 copy-start.3
  0.7 0.0 copy-start.2
  0.7 47.3 %rows.1 = (f32[4,32,1536]{2,1,0:T(8,128)}, f32[128,16,128]{2,1,0:T(8,128)}) custom-call(s32[640]{0:T(1024)} %wave_hbm.3, s32[128]{0:T(128)} %band_hbm.3, s32[64]{0:T(128)} %len_hbm.3, f32[64]{0:T(128)} %gauss_hbm.1, f32[40,2,2,2,1281]{4,3,2,1,0:T(2,128)} %spec_hbm.1, f32[40,64,1281]{2,1,0:T(8,128)} %leg_hbm.3), custom_call_target="tpu_custom_call" | custom-call | tf_op jit(solution)/shard_map/rows/pallas_call | solution.py:575
  48.0 0.0 copy-done.4
  48.0 0.0 copy-done.3
  48.0 0.0 copy-done.2
  48.0 0.0 copy-start
  48.0 1.2 %copy-done = f32[128,16,128]{2,1,0:T(8,128)S(1)} copy-done((f32[128,16,128]{2,1,0:T(8,128)S(1)}, f32[128,16,128]{2,1,0:T(8,128)}, u32[]{:S(2)}) %copy-start) | copy-done | bytes 1048600
  49.2 0.0 copy-start.1
  49.2 1.1 %copy-done.1 = f32[4,32,1536]{2,1,0:T(8,128)S(1)} copy-done((f32[4,32,1536]{2,1,0:T(8,128)S(1)}, f32[4,32,1536]{2,1,0:T(8,128)}, u32[]{:S(2)}) %copy-start.1) | copy-done | bytes 786456
  50.4 8.9 %direct.1 = (f32[40,5,2,2,1281]{4,3,2,1,0:T(2,128)}, f32[1,2,16,5248]{3,2,1,0:T(8,128)}) custom-call(s32[640]{0:T(1024)S(1)} %copy-done.2, s32[128]{0:T(128)S(1)} %copy-done.3, s32[64]{0:T(128)S(1)} %copy-done.4, f32[128,16,128]{2,1,0:T(8,128)S(1)} %copy-done, f32[4,32,1536]{2,1,0:T(8,128)S(1)} %copy-done.1, f32[40,64,1281]{2,1,0:T(8,128)} %leg_hbm.3), custom_call_target="tpu_custom_call" | custom-call | tf_op jit(solution)/shard_map/direct/pallas_call | solution.py:629
Async XLA Ops:
  0.6 47.4 %copy-start.4 = (s32[64]{0:T(128)S(1)}, s32[64]{0:T(128)}, u32[]{:S(2)}) copy-start(s32[64]{0:T(128)} %len_hbm.3) | copy-start | bytes 772
  0.6 47.4 %copy-start.3 = (s32[128]{0:T(128)S(1)}, s32[128]{0:T(128)}, u32[]{:S(2)}) copy-start(s32[128]{0:T(128)} %band_hbm.3) | copy-start | bytes 1540
  0.7 47.4 %copy-start.2 = (s32[640]{0:T(1024)S(1)}, s32[640]{0:T(1024)}, u32[]{:S(2)}) copy-start(s32[640]{0:T(1024)} %wave_hbm.3) | copy-start | bytes 7684
  48.0 1.2 %copy-start = (f32[128,16,128]{2,1,0:T(8,128)S(1)}, f32[128,16,128]{2,1,0:T(8,128)}, u32[]{:S(2)}) copy-start(f32[128,16,128]{2,1,0:T(8,128)} %get-tuple-element.6.in_hbm) | copy-start | bytes 3145732
  49.2 1.1 %copy-start.1 = (f32[4,32,1536]{2,1,0:T(8,128)S(1)}, f32[4,32,1536]{2,1,0:T(8,128)}, u32[]{:S(2)}) copy-start(f32[4,32,1536]{2,1,0:T(8,128)} %get-tuple-element.7.segs_hbm) | copy-start | bytes 2359300
